TPU v7x, 32 devices: a whole 2x2x4 slice. The times are simulated.
32 devices in a mesh: blk: 4 (over y, x), rep: 8 (over z, core).
Axes of the slice: x: 2, y: 2, z: 4, core: 2. Of those that a mesh axis runs over, the one named last changes fastest.
Arguments:
- scores: bfloat16 [8192, 256], P(('blk', 'rep')), may hold values from 0 to 2
- tiles: bfloat16 [64, 4, 16, 128, 128], P(('blk', 'rep')), may hold values from 0 to 0.125
- cols: int32 [64, 4, 16], P(('blk', 'rep')), may hold values from 0 to 15, as said below
- counts: int32 [64, 4], P(('blk', 'rep')), may hold values from 1 to 16
- seeds: int32 [256, 16], replicated, may hold values from 0 to 8191
Outputs:
- diffused: bfloat16 [8192, 256], P(('blk', 'rep'))
Inputs may be any that keep to these rules, and one draw needn't show every extreme that they name: `cols`: within one row block and column panel the first counts entries are distinct.
All inputs are finite; a program needn't handle non-finite values.
Results may differ from a plain program's by a relative error of at most 0.0029.
Values may be sent and summed in bfloat16 or wider, within the bound.
No kernel may reach another device: no remote copies, remote signals or barrier semaphores. Data moves between devices by JAX's collectives and lax.ppermute only.
A program may use at most 128 MiB of HBM per device.

v0:
```python
import jax
import jax.numpy as jnp
from jax import lax
from jax.sharding import PartitionSpec as P

HOPS = 2


def shifted(value, axis, by):
    count = lax.axis_size(axis)
    return lax.ppermute(value, axis, [(i, (i + by) % count) for i in range(count)])


def per_device(scores, tiles, cols, counts, seeds):
    rows_dev = scores.shape[0]
    queries = scores.shape[1]
    blocks_dev = tiles.shape[0]
    panels = tiles.shape[1]
    slot_count = tiles.shape[2]
    block_size = tiles.shape[3]
    members = lax.axis_size("rep")
    own_panel = lax.axis_index("blk")
    member_index = lax.axis_index("rep")
    first_row = (own_panel * members + member_index) * rows_dev
    node_ids = first_row + jnp.arange(rows_dev, dtype=jnp.int32)
    restart = jnp.sum((node_ids[:, None, None] == seeds[None, :, :]).astype(jnp.float32), axis=2)

    def add_panel(summed, gathered, panel_index):
        panel_blocks = gathered.reshape(-1, block_size, queries)
        where_cols = lax.dynamic_index_in_dim(cols, panel_index, 1, keepdims=False)
        allowed = lax.dynamic_index_in_dim(counts, panel_index, 1, keepdims=False)
        weights_all = lax.dynamic_index_in_dim(tiles, panel_index, 1, keepdims=False)
        picked = panel_blocks[where_cols]
        active = jnp.arange(slot_count, dtype=jnp.int32)[None, :] < allowed[:, None]
        picked = jnp.where(active[:, :, None, None], picked, jnp.zeros((), jnp.bfloat16))
        return summed + jnp.einsum(
            "ikab,ikbq->iaq", weights_all, picked, preferred_element_type=jnp.float32
        )

    current = scores
    for hop_index in range(HOPS):
        gathered = lax.all_gather(current, "rep", axis=0, tiled=True)
        summed = jnp.zeros((blocks_dev, block_size, queries), jnp.float32)
        summed = add_panel(summed, gathered, own_panel)

        def onward(m, carried):
            running, visitor = carried
            visitor = shifted(visitor, "blk", 1)
            return (add_panel(running, visitor, (own_panel - m) % panels), visitor)

        summed, unused_onward = lax.fori_loop(1, panels, onward, (summed, gathered))
        current = (0.9 * summed.reshape(rows_dev, queries) + restart).astype(jnp.bfloat16)
    return current


def solution(mesh):
    return jax.shard_map(
        per_device,
        mesh=mesh,
        in_specs=(
            P(("blk", "rep"), None),
            P(("blk", "rep"), None, None, None, None),
            P(("blk", "rep"), None, None),
            P(("blk", "rep"), None),
            P(),
        ),
        out_specs=P(("blk", "rep"), None),
        check_vma=False,
    )
```

profile of v0, /device:TPU:0, one launch (start us, length us, event | category | flops | bytes accessed | tf_op | source)
XLA Modules:
  0.0 249.7 jit_solution(9048857441915187566)
XLA Ops:
  10.4 4.7 %copy.13 = bf16[2,4,16,128,128]{4,3,2,0,1:T(8,128)(2,1)} copy(bf16[2,4,16,128,128]{4,3,2,1,0:T(8,128)(2,1)} %param.10) | data formatting | bytes 8388608 | tf_op jit(solution)/shard_map/while | solution.py:51
  15.2 1.5 convert_reduce_fusion
  16.8 17.0 %all-gather.3.cloned.1.call-done = bf16[2048,256]{1,0:T(8,128)(2,1)} async-done(((bf16[256,256]{1,0:T(8,128)(2,1)}), bf16[2048,256]{1,0:T(8,128)(2,1)}) %all-gather.3.cloned.1.call-update) | async-done | bytes 1048592 | tf_op jit(solution)/shard_map/all_gather | solution.py:42
  33.8 3.2 %gather_fusion.2 = bf16[32,128,256]{2,1,0:T(8,128)(2,1)} fusion(bf16[16,128,256]{2,1,0:T(8,128)(2,1)} %bitcast.86, s32[1024]{0:T(1024)S(1)} %pad_clamp_fusion.2), kind=kCustom, calls=%fused_computation.2 | custom fusion | bytes 4194432 | tf_op jit(solution)/shard_map/gather | solution.py:33
  37.0 3.2 %fusion.36 = f32[2,128,256]{2,1,0:T(8,128)} fusion(bf16[2,16,128,256]{3,2,1,0:T(8,128)(2,1)} %bitcast.89, pred[2,16]{1,0:T(4,128)(4,1)S(1)} %iota_compare_fusion.2, bf16[2,4,16,128,128]{4,3,2,1,0:T(8,128)(2,1)} %param.10, s32[]{:T(128)S(6)} %select_n.144), kind=kOutput, calls=%fused_computation.41 | convolution fusion | flops 269484032 | bytes 3407908 | tf_op jit(solution)/shard_map/ikab,ikbq->iaq/dot_general | solution.py:36
  40.2 85.9 %while.34 = (s32[]{:T(128)}, f32[2,128,256]{2,1,0:T(8,128)}, bf16[2048,256]{1,0:T(8,128)(2,1)S(1)}, s32[]{:T(128)}, bf16[2,4,16,128,128]{4,3,2,0,1:T(8,128)(2,1)...) while((s32[]{:T(128)}, f32[2,128,256]{2,1,0:T(8,128)}, ...), condition=%wide.region_1.2_spmd, body=%wide.region_0.0_spmd.sunk | while | flops 269550720 | bytes 14161044 | solution.py:51
  40.2 1.5 collective-permute-start
  41.9 24.6 %collective-permute-done = bf16[2048,256]{1,0:T(8,128)(2,1)S(1)} collective-permute-done((bf16[2048,256]{1,0:T(8,128)(2,1)S(1)}, bf16[2048,256]{1,0:T(8,128)(2,1)S(1)}, u32[]{:S(2)}, u32[]{:S(2)}) %collective-permute-start) | collective-permute-done | bytes 1048608 | tf_op jit(solution)/shard_map/while/body/eval_jaxpr/ppermute | solution.py:11
  67.1 2.5 fusion.65
  70.5 24.6 %collective-permute-done = bf16[2048,256]{1,0:T(8,128)(2,1)S(1)} collective-permute-done((bf16[2048,256]{1,0:T(8,128)(2,1)S(1)}, bf16[2048,256]{1,0:T(8,128)(2,1)S(1)}, u32[]{:S(2)}, u32[]{:S(2)}) %collective-permute-start) | collective-permute-done | bytes 1048608 | tf_op jit(solution)/shard_map/while/body/eval_jaxpr/ppermute | solution.py:11
  95.8 2.5 fusion.65
  98.7 24.2 %collective-permute-done = bf16[2048,256]{1,0:T(8,128)(2,1)S(1)} collective-permute-done((bf16[2048,256]{1,0:T(8,128)(2,1)S(1)}, bf16[2048,256]{1,0:T(8,128)(2,1)S(1)}, u32[]{:S(2)}, u32[]{:S(2)}) %collective-permute-start) | collective-permute-done | bytes 1048608 | tf_op jit(solution)/shard_map/while/body/eval_jaxpr/ppermute | solution.py:11
  123.6 2.5 fusion.65
  127.8 21.0 %all-gather.5.cloned.1.call-done = bf16[2048,256]{1,0:T(8,128)(2,1)} async-done(((bf16[256,256]{1,0:T(8,128)(2,1)}), bf16[2048,256]{1,0:T(8,128)(2,1)}) %all-gather.5.cloned.1.call-update) | async-done | bytes 1048592 | tf_op jit(solution)/shard_map/all_gather | solution.py:42
  148.9 3.2 %gather_fusion.3 = bf16[32,128,256]{2,1,0:T(8,128)(2,1)} fusion(bf16[16,128,256]{2,1,0:T(8,128)(2,1)} %bitcast.87, s32[1024]{0:T(1024)S(1)} %pad_clamp_fusion.2), kind=kCustom, calls=%fused_computation.3 | custom fusion | bytes 4194432 | tf_op jit(solution)/shard_map/gather | solution.py:33
  152.1 3.2 %fusion.39 = f32[2,128,256]{2,1,0:T(8,128)} fusion(bf16[2,16,128,256]{3,2,1,0:T(8,128)(2,1)} %bitcast.88, pred[2,16]{1,0:T(4,128)(4,1)S(1)} %iota_compare_fusion.2, bf16[2,4,16,128,128]{4,3,2,1,0:T(8,128)(2,1)} %param.10, s32[]{:T(128)S(6)} %select_n.144), kind=kOutput, calls=%fused_computation.42 | convolution fusion | flops 269484032 | bytes 3407908 | tf_op jit(solution)/shard_map/ikab,ikbq->iaq/dot_general | solution.py:36
  155.3 85.9 %while.35 = (s32[]{:T(128)}, f32[2,128,256]{2,1,0:T(8,128)}, bf16[2048,256]{1,0:T(8,128)(2,1)S(1)}, s32[]{:T(128)}, bf16[2,4,16,128,128]{4,3,2,0,1:T(8,128)(2,1)...) while((s32[]{:T(128)}, f32[2,128,256]{2,1,0:T(8,128)}, ...), condition=%wide.region_4.5_spmd, body=%wide.region_3.4_spmd.sunk | while | flops 269550720 | bytes 14161044 | solution.py:51
  155.3 1.5 collective-permute-start.1
  157.0 24.6 %collective-permute-done.1 = bf16[2048,256]{1,0:T(8,128)(2,1)S(1)} collective-permute-done((bf16[2048,256]{1,0:T(8,128)(2,1)S(1)}, bf16[2048,256]{1,0:T(8,128)(2,1)S(1)}, u32[]{:S(2)}, u32[]{:S(2)}) %collective-permute-start.1) | collective-permute-done | bytes 1048608 | tf_op jit(solution)/shard_map/while/body/eval_jaxpr/ppermute | solution.py:11
  182.2 2.5 fusion.69
  185.6 24.6 %collective-permute-done.1 = bf16[2048,256]{1,0:T(8,128)(2,1)S(1)} collective-permute-done((bf16[2048,256]{1,0:T(8,128)(2,1)S(1)}, bf16[2048,256]{1,0:T(8,128)(2,1)S(1)}, u32[]{:S(2)}, u32[]{:S(2)}) %collective-permute-start.1) | collective-permute-done | bytes 1048608 | tf_op jit(solution)/shard_map/while/body/eval_jaxpr/ppermute | solution.py:11
  210.9 2.5 fusion.69
  213.7 24.2 %collective-permute-done.1 = bf16[2048,256]{1,0:T(8,128)(2,1)S(1)} collective-permute-done((bf16[2048,256]{1,0:T(8,128)(2,1)S(1)}, bf16[2048,256]{1,0:T(8,128)(2,1)S(1)}, u32[]{:S(2)}, u32[]{:S(2)}) %collective-permute-start.1) | collective-permute-done | bytes 1048608 | tf_op jit(solution)/shard_map/while/body/eval_jaxpr/ppermute | solution.py:11
  238.7 2.5 fusion.69
  (69 shorter events, 14.1 us)
Async XLA Ops:
  6.5 27.3 %all-gather.3.cloned.1.call-start = ((), (), s32[]{:S(2)}) async-start(), calls=%async_computation | async-start | bytes 1179648 | tf_op jit(solution)/shard_map/all_gather | solution.py:42
  7.3 141.6 %all-gather.5.cloned.1.call-start = ((), (), s32[]{:S(2)}) async-start(), calls=%async_computation.1 | async-start | bytes 1179648 | tf_op jit(solution)/shard_map/all_gather | solution.py:42
  10.4 4.7 %copy-start.2 = (s32[256,16]{0,1:T(8,128)S(1)}, s32[256,16]{0,1:T(8,128)}, u32[]{:S(2)}) copy-start(s32[256,16]{0,1:T(8,128)} %param.13) | copy-start | bytes 49156
  37.0 3.2 %copy-start = (bf16[2048,256]{1,0:T(8,128)(2,1)S(1)}, bf16[2048,256]{1,0:T(8,128)(2,1)}, u32[]{:S(2)}) copy-start(bf16[2048,256]{1,0:T(8,128)(2,1)} %all-gather.3.cloned.1.call-done) | copy-start | bytes 3145732
  40.2 26.2 %collective-permute-start = (bf16[2048,256]{1,0:T(8,128)(2,1)S(1)}, bf16[2048,256]{1,0:T(8,128)(2,1)S(1)}, u32[]{:S(2)}, u32[]{:S(2)}) collective-permute-start(bf16[2048,256]{1,0:T(8,128)(2,1)S(1)} %get-tuple-element.516), channel_id=1, source_target_pairs={{0,8},{8,16},{16,24},{24,0},{1,9},{9,17},{17,25},{25,1},{2,10},{10... | collective-permute-start | bytes 3145736 | tf_op jit(solution)/shard_map/while/body/eval_jaxpr/ppermute | solution.py:11
  69.7 25.4 %collective-permute-start = (bf16[2048,256]{1,0:T(8,128)(2,1)S(1)}, bf16[2048,256]{1,0:T(8,128)(2,1)S(1)}, u32[]{:S(2)}, u32[]{:S(2)}) collective-permute-start(bf16[2048,256]{1,0:T(8,128)(2,1)S(1)} %get-tuple-element.516), channel_id=1, source_target_pairs={{0,8},{8,16},{16,24},{24,0},{1,9},{9,17},{17,25},{25,1},{2,10},{10... | collective-permute-start | bytes 3145736 | tf_op jit(solution)/shard_map/while/body/eval_jaxpr/ppermute | solution.py:11
  98.4 24.5 %collective-permute-start = (bf16[2048,256]{1,0:T(8,128)(2,1)S(1)}, bf16[2048,256]{1,0:T(8,128)(2,1)S(1)}, u32[]{:S(2)}, u32[]{:S(2)}) collective-permute-start(bf16[2048,256]{1,0:T(8,128)(2,1)S(1)} %get-tuple-element.516), channel_id=1, source_target_pairs={{0,8},{8,16},{16,24},{24,0},{1,9},{9,17},{17,25},{25,1},{2,10},{10... | collective-permute-start | bytes 3145736 | tf_op jit(solution)/shard_map/while/body/eval_jaxpr/ppermute | solution.py:11
  152.1 3.2 %copy-start.1 = (bf16[2048,256]{1,0:T(8,128)(2,1)S(1)}, bf16[2048,256]{1,0:T(8,128)(2,1)}, u32[]{:S(2)}) copy-start(bf16[2048,256]{1,0:T(8,128)(2,1)} %all-gather.5.cloned.1.call-done) | copy-start | bytes 3145732
  155.3 26.2 %collective-permute-start.1 = (bf16[2048,256]{1,0:T(8,128)(2,1)S(1)}, bf16[2048,256]{1,0:T(8,128)(2,1)S(1)}, u32[]{:S(2)}, u32[]{:S(2)}) collective-permute-start(bf16[2048,256]{1,0:T(8,128)(2,1)S(1)} %get-tuple-element.549), channel_id=1, source_target_pairs={{0,8},{8,16},{16,24},{24,0},{1,9},{9,17},{17,25},{25,1},{2,10},{10... | collective-permute-start | bytes 3145736 | tf_op jit(solution)/shard_map/while/body/eval_jaxpr/ppermute | solution.py:11
  184.8 25.4 %collective-permute-start.1 = (bf16[2048,256]{1,0:T(8,128)(2,1)S(1)}, bf16[2048,256]{1,0:T(8,128)(2,1)S(1)}, u32[]{:S(2)}, u32[]{:S(2)}) collective-permute-start(bf16[2048,256]{1,0:T(8,128)(2,1)S(1)} %get-tuple-element.549), channel_id=1, source_target_pairs={{0,8},{8,16},{16,24},{24,0},{1,9},{9,17},{17,25},{25,1},{2,10},{10... | collective-permute-start | bytes 3145736 | tf_op jit(solution)/shard_map/while/body/eval_jaxpr/ppermute | solution.py:11
  213.5 24.5 %collective-permute-start.1 = (bf16[2048,256]{1,0:T(8,128)(2,1)S(1)}, bf16[2048,256]{1,0:T(8,128)(2,1)S(1)}, u32[]{:S(2)}, u32[]{:S(2)}) collective-permute-start(bf16[2048,256]{1,0:T(8,128)(2,1)S(1)} %get-tuple-element.549), channel_id=1, source_target_pairs={{0,8},{8,16},{16,24},{24,0},{1,9},{9,17},{17,25},{25,1},{2,10},{10... | collective-permute-start | bytes 3145736 | tf_op jit(solution)/shard_map/while/body/eval_jaxpr/ppermute | solution.py:11
Sparse Core Ops, SparseCore 0:
  9.0 24.7 all-gather.2
  128.0 20.8 all-gather.4
where the time goes:
time: 250 us
  waiting for transfers between devices  186 us (74%)
  matrix products  21.4 us (9%)
  local copies, waits for them, and re-layouts  19.3 us (8%)
  between operations  13.5 us (5%)
  other arithmetic  5.44 us (2%)
  starting transfers between devices  4.28 us (2%)
    ppermute x6, waiting for transfers between devices, shifted(): lax.ppermute(value, axis, [(i, (i + by) % count) for i in range(count)])  147 us
    all_gather x2, waiting for transfers between devices, per_device(): gathered = lax.all_gather(current, 'rep', axis=0, tiled=True)  38.1 us
    dot_general x8, matrix products, add_panel(): jnp.einsum('ikab,ikbq->iaq', weights_all, picked, preferred_element_type=...  21.4 us
    gather x8, local copies, waits for them, and re-layouts, add_panel(): picked = panel_blocks[where_cols]  10.5 us
    while x3, local copies, waits for them, and re-layouts, per_device(): summed, unused_onward = lax.fori_loop(1, panels, onward, (summed, gathered))  6.19 us
  transfers between devices with their start and end apart: 8, of which 8 were waited for; matrix products, arithmetic and copies ran while one was open for 4% of the time, Pallas kernels for 0%

commit v1 on v0

v1 whole, which is shorter than its diff:
```python
import functools
import math

import jax
import jax.numpy as jnp
from jax import lax
from jax.experimental import pallas as pl
from jax.experimental.pallas import tpu as pltpu
from jax.sharding import PartitionSpec as P

HOPS = 2
AXES = ("blk", "rep")


def expand_kernel(place, cols, counts, tiles, own, other, *, side):
    blocks_dev, panels, _, bs, _ = tiles.shape
    own[...] = jnp.zeros_like(own)
    other[...] = jnp.zeros_like(other)
    y, x, z, core = place[0], place[1], place[2], place[3]

    def panel_step(step, carry):
        i = step // panels
        p = step % panels
        down = lax.rem(y - p // side + side, side)
        across = lax.rem(x - p % side + side, side)

        def slot_step(k, carry):
            block = cols[step, k]
            source = block // blocks_dev
            half = block % blocks_dev
            source_core = source % 2
            first = jnp.where(source_core == 0, down, across)
            second = jnp.where(source_core == 0, across, down)
            piece = ((z ^ (source // 2)) * side + first) * side + second
            tile = tiles[i, p, k]
            rows = pl.ds(pl.multiple_of(i * bs, bs), bs)
            lanes = pl.ds(pl.multiple_of(half * bs, bs), bs)

            @pl.when(source_core == core)
            def _():
                own[piece, rows, lanes] = tile

            @pl.when(source_core != core)
            def _():
                other[piece, rows, lanes] = tile

            return carry

        return lax.fori_loop(0, counts[step], slot_step, carry)

    lax.fori_loop(0, blocks_dev * panels, panel_step, 0)


def expand(place, cols, counts, tiles, side, pieces):
    blocks_dev, panels, slots, bs, _ = tiles.shape
    rows = blocks_dev * bs
    shape = jax.ShapeDtypeStruct((pieces, rows, rows), tiles.dtype)
    return pl.pallas_call(
        functools.partial(expand_kernel, side=side),
        out_shape=(shape, shape),
        in_specs=[pl.BlockSpec(memory_space=pltpu.SMEM)] * 3
        + [pl.BlockSpec(memory_space=pltpu.VMEM)],
        out_specs=(pl.BlockSpec(memory_space=pltpu.VMEM),) * 2,
        compiler_params=pltpu.CompilerParams(vmem_limit_bytes=48 << 20),
        cost_estimate=pl.CostEstimate(flops=0, bytes_accessed=2 * tiles.size * 2, transcendentals=0),
        name="expand_blocks",
    )(place, cols.reshape(-1, slots), counts.reshape(-1), tiles)


def permutes(side, depth):
    places = [
        (y, x, z, c) for y in range(side) for x in range(side) for z in range(depth) for c in range(2)
    ]

    def index(y, x, z, c):
        return (((y % side) * side + x % side) * depth + z) * 2 + c

    def pairs(move):
        return [(index(*place), index(*move(*place))) for place in places]

    along = {k: pairs(lambda y, x, z, c: (y, x, z ^ k, c)) for k in range(1, depth)}
    first = {
        j: pairs(lambda y, x, z, c: (y, x + j, z, c) if c else (y + j, x, z, c)) for j in range(1, side)
    }
    second = {
        j: pairs(lambda y, x, z, c: (y + j, x, z, c) if c else (y, x + j, z, c)) for j in range(1, side)
    }
    return along, first, second, pairs(lambda y, x, z, c: (y, x, z, 1 - c))


def per_device(scores, tiles, cols, counts, seeds):
    rows_dev = scores.shape[0]
    members = lax.axis_size("rep")
    side = math.isqrt(lax.axis_size("blk"))
    depth = members // 2
    panel = lax.axis_index("blk")
    member = lax.axis_index("rep")
    place = jnp.stack([panel // side, panel % side, member // 2, member % 2]).astype(jnp.int32)
    along, first, second, across = permutes(side, depth)

    def send(value, pairs):
        return lax.ppermute(value, AXES, pairs)

    own, other = expand(place, cols, counts, tiles, side, depth * side * side)
    partner = send(other, across)

    node_ids = (panel * members + member) * rows_dev + jnp.arange(rows_dev, dtype=jnp.int32)
    restart = jnp.sum((node_ids[:, None, None] == seeds[None, :, :]).astype(jnp.float32), axis=2)

    current = scores
    for hop_index in range(HOPS):
        arrived = {}
        for d in range(depth):
            column = current if d == 0 else send(current, along[d])
            arrived[d, 0, 0] = column
        for d in range(depth):
            for a in range(1, side):
                arrived[d, a, 0] = send(arrived[d, 0, 0], first[a])
            for b in range(1, side):
                for a in range(side):
                    arrived[d, a, b] = send(arrived[d, a, 0], second[b])
        mine = jnp.zeros((rows_dev, scores.shape[1]), jnp.float32)
        theirs = jnp.zeros((rows_dev, scores.shape[1]), jnp.float32)
        for (d, a, b), piece in arrived.items():
            at = (d * side + a) * side + b
            theirs += jnp.dot(partner[at], piece, preferred_element_type=jnp.float32)
        for (d, a, b), piece in arrived.items():
            at = (d * side + a) * side + b
            mine += jnp.dot(own[at], piece, preferred_element_type=jnp.float32)
        summed = mine + send(theirs, across)
        current = (0.9 * summed + restart).astype(jnp.bfloat16)
    return current


def solution(mesh):
    return jax.shard_map(
        per_device,
        mesh=mesh,
        in_specs=(
            P(AXES, None),
            P(AXES, None, None, None, None),
            P(AXES, None, None),
            P(AXES, None),
            P(),
        ),
        out_specs=P(AXES, None),
        check_vma=False,
    )
```

time: 250 us -> 81 us (0.32)
  waiting for transfers between devices: 186 us -> 25.1 us
  starting transfers between devices: 4.28 us -> 32.6 us
  local copies, waits for them, and re-layouts: 19.3 us -> 2.79 us
  between operations: 13.5 us -> 0.76 us
  matrix products: 21.4 us -> 12.5 us
  Pallas kernels: 0 us -> 5.34 us
  other arithmetic: 5.44 us -> 1.6 us
    ppermute x6 -> x33, waiting for transfers between devices: 147 us -> 25.1 us  [send(): return lax.ppermute(value, AXES, pairs)]
    all_gather x2 -> x0, waiting for transfers between devices: 38.1 us -> none  [per_device(): gathered = lax.all_gather(current, 'rep', axis=0, tiled=True)]
    ppermute x6 -> x33, starting transfers between devices: 4.24 us -> 32.6 us  [send(): return lax.ppermute(value, AXES, pairs)]
    gather x8 -> x0, local copies, waits for them, and re-layouts: 10.5 us -> none  [add_panel(): picked = panel_blocks[where_cols]]
    dot_general x8 -> x64, matrix products: 21.4 us -> 12.5 us  [the longest x32 6.6 us: per_device(): mine += jnp.dot(own[at], piece, preferred_element_type=jnp.float32)]
    while x9 -> x0, local copies, waits for them, and re-layouts: 6.6 us -> none  [the longest x3 6.19 us: per_device(): summed, unused_onward = lax.fori_loop(1, panels, onward, (summed, gathered))]
    pallas_call x0 -> x1, Pallas kernels: none -> 5.34 us  [expand(): pl.pallas_call(functools.partial(expand_kernel, side=side), out_shape=(sh...]
  transfers between devices with their start and end apart: 8 -> 33, of which waited for: 8 -> 13; matrix products, arithmetic and copies ran while one was open for 4% -> 17% of each run, Pallas kernels for 0% -> 7%
where the time goes in v1:
time: 81 us; the launch traced here: 80.7 us
  starting transfers between devices  32.6 us (40%)
  waiting for transfers between devices  25.1 us (31%)
  matrix products  12.5 us (15%)
  Pallas kernels  5.34 us (7%)
  local copies, waits for them, and re-layouts  2.79 us (3%)
  other arithmetic  1.6 us (2%)
    ppermute x33, starting transfers between devices, send(): return lax.ppermute(value, AXES, pairs)  32.6 us
    ppermute x33, waiting for transfers between devices, send(): return lax.ppermute(value, AXES, pairs)  25.1 us
    dot_general x32, matrix products, per_device(): mine += jnp.dot(own[at], piece, preferred_element_type=jnp.float32)  6.6 us
    dot_general x32, matrix products, per_device(): theirs += jnp.dot(partner[at], piece, preferred_element_type=jnp.float32)  5.93 us
    pallas_call x1, Pallas kernels, expand(): pl.pallas_call(functools.partial(expand_kernel, side=side), out_shape=(sh...  5.34 us
    unnamed x8, local copies, waits for them, and re-layouts  2.03 us
  transfers between devices with their start and end apart: 33, of which 13 were waited for; matrix products, arithmetic and copies ran while one was open for 17% of the time, Pallas kernels for 7%

profile of v1, /device:TPU:0, one launch (start us, length us, event | category | flops | bytes accessed | tf_op | source)
XLA Modules:
  0.0 80.7 jit_solution(3569734184820967791)
XLA Ops:
  0.0 3.0 %collective-permute-start = (bf16[256,256]{1,0:T(8,128)(2,1)}, bf16[256,256]{1,0:T(8,128)(2,1)S(1)}, u32[]{:S(2)}, u32[]{:S(2)}) collective-permute-start(bf16[256,256]{1,0:T(8,128)(2,1)} %param.5), channel_id=1, source_target_pairs={{0,2},{1,3},{2,0},{3,1},{4,6},{5,7},{6,4},{7,5},{8,10},{9,11},{10,... | collective-permute-start | bytes 393224 | tf_op jit(solution)/shard_map/ppermute | solution.py:102
  3.0 1.5 %collective-permute-start.4 = (bf16[256,256]{1,0:T(8,128)(2,1)}, bf16[256,256]{1,0:T(8,128)(2,1)S(1)}, u32[]{:S(2)}, u32[]{:S(2)}) collective-permute-start(bf16[256,256]{1,0:T(8,128)(2,1)} %param.5), channel_id=1, source_target_pairs={{0,8},{1,17},{2,10},{3,19},{4,12},{5,21},{6,14},{7,23},{8,0},{9,25... | collective-permute-start | bytes 393224 | tf_op jit(solution)/shard_map/ppermute | solution.py:102
  4.5 1.5 %collective-permute-start.3 = (bf16[256,256]{1,0:T(8,128)(2,1)}, bf16[256,256]{1,0:T(8,128)(2,1)S(1)}, u32[]{:S(2)}, u32[]{:S(2)}) collective-permute-start(bf16[256,256]{1,0:T(8,128)(2,1)} %param.5), channel_id=1, source_target_pairs={{0,16},{1,9},{2,18},{3,11},{4,20},{5,13},{6,22},{7,15},{8,24},{9,1... | collective-permute-start | bytes 393224 | tf_op jit(solution)/shard_map/ppermute | solution.py:102
  6.0 2.5 %collective-permute-start.2 = (bf16[256,256]{1,0:T(8,128)(2,1)}, bf16[256,256]{1,0:T(8,128)(2,1)S(1)}, u32[]{:S(2)}, u32[]{:S(2)}) collective-permute-start(bf16[256,256]{1,0:T(8,128)(2,1)} %param.5), channel_id=1, source_target_pairs={{0,6},{1,7},{2,4},{3,5},{4,2},{5,3},{6,0},{7,1},{8,14},{9,15},{10,... | collective-permute-start | bytes 393224 | tf_op jit(solution)/shard_map/ppermute | solution.py:102
  10.2 5.3 %expand_blocks.1 = (bf16[16,256,256]{2,1,0:T(8,128)(2,1)S(1)}, bf16[16,256,256]{2,1,0:T(8,128)(2,1)S(1)}) custom-call(s32[4]{0:T(128)S(1)} %pad_add_fusion.place, s32[8,16]{1,0:T(8,128)S(1)} %bitcast.213, s32[8]{0:T(128)S(1)} %reshape.12.counts, bf16[2,4,16,128,128]{4,3,2,1,0:T(8,128)(2,1)} %tiles.1), custom_call_target="tpu_custom_call" | custom-call | bytes 8388608 | tf_op jit(solution)/shard_map/expand_blocks/pallas_call | solution.py:58
  15.5 1.3 %copy-done.1 = bf16[16,256,256]{2,1,0:T(8,128)(2,1)} copy-done((bf16[16,256,256]{2,1,0:T(8,128)(2,1)}, bf16[16,256,256]{2,1,0:T(8,128)(2,1)S(1)}, u32[]{:S(2)}) %copy-start.1) | copy-done | bytes 2097176
  17.1 1.5 %convert_reduce_fusion = f32[256,256]{1,0:T(8,128)S(1)} fusion(s32[256,16]{0,1:T(8,128)S(1)} %copy-done.3, s32[256]{0:T(256)S(1)} %iota_add_fusion), kind=kLoop, calls=%fused_computation | loop fusion | flops 3080192 | bytes 279552 | tf_op jit(solution)/shard_map/reduce_sum | solution.py:108
  19.5 2.1 %collective-permute-start.5 = (bf16[256,256]{1,0:T(8,128)(2,1)S(1)}, bf16[256,256]{1,0:T(8,128)(2,1)S(1)}, u32[]{:S(2)}, u32[]{:S(2)}) collective-permute-start(bf16[256,256]{1,0:T(8,128)(2,1)S(1)} %collective-permute-done.3), channel_id=1, source_target_pairs={{0,8},{1,17},{2,10},{3,19},{4,12},{5,21},{6,14},{7,23},{8,0},{9,25... | collective-permute-start | bytes 393224 | tf_op jit(solution)/shard_map/ppermute | solution.py:102
  22.0 3.1 %collective-permute-done.7 = bf16[256,256]{1,0:T(8,128)(2,1)S(1)} collective-permute-done((bf16[256,256]{1,0:T(8,128)(2,1)S(1)}, bf16[256,256]{1,0:T(8,128)(2,1)S(1)}, u32[]{:S(2)}, u32[]{:S(2)}) %collective-permute-start.7) | collective-permute-done | bytes 131104 | tf_op jit(solution)/shard_map/ppermute | solution.py:102
  25.6 2.0 %collective-permute-start.13 = (bf16[256,256]{1,0:T(8,128)(2,1)S(1)}, bf16[256,256]{1,0:T(8,128)(2,1)S(1)}, u32[]{:S(2)}, u32[]{:S(2)}) collective-permute-start(bf16[256,256]{1,0:T(8,128)(2,1)S(1)} %collective-permute-done.2), channel_id=1, source_target_pairs={{0,8},{1,17},{2,10},{3,19},{4,12},{5,21},{6,14},{7,23},{8,0},{9,25... | collective-permute-start | bytes 393224 | tf_op jit(solution)/shard_map/ppermute | solution.py:102
  27.7 1.2 %collective-permute-done.10 = bf16[256,256]{1,0:T(8,128)(2,1)S(1)} collective-permute-done((bf16[256,256]{1,0:T(8,128)(2,1)S(1)}, bf16[256,256]{1,0:T(8,128)(2,1)S(1)}, u32[]{:S(2)}, u32[]{:S(2)}) %collective-permute-start.10) | collective-permute-done | bytes 131104 | tf_op jit(solution)/shard_map/ppermute | solution.py:102
  31.8 3.6 %collective-permute-done.12 = bf16[256,256]{1,0:T(8,128)(2,1)S(1)} collective-permute-done((bf16[256,256]{1,0:T(8,128)(2,1)S(1)}, bf16[256,256]{1,0:T(8,128)(2,1)S(1)}, u32[]{:S(2)}, u32[]{:S(2)}) %collective-permute-start.12) | collective-permute-done | bytes 131104 | tf_op jit(solution)/shard_map/ppermute | solution.py:102
  35.5 2.1 %collective-permute-start.14 = (bf16[256,256]{1,0:T(8,128)(2,1)S(1)}, bf16[256,256]{1,0:T(8,128)(2,1)S(1)}, u32[]{:S(2)}, u32[]{:S(2)}) collective-permute-start(bf16[256,256]{1,0:T(8,128)(2,1)S(1)} %collective-permute-done.12), channel_id=1, source_target_pairs={{0,8},{1,17},{2,10},{3,19},{4,12},{5,21},{6,14},{7,23},{8,0},{9,25... | collective-permute-start | bytes 393224 | tf_op jit(solution)/shard_map/ppermute | solution.py:102
  42.4 1.1 %collective-permute-done.16 = f32[256,256]{1,0:T(8,128)S(1)} collective-permute-done((f32[256,256]{1,0:T(8,128)S(1)}, f32[256,256]{1,0:T(8,128)S(1)}, u32[]{:S(2)}, u32[]{:S(2)}) %collective-permute-start.16) | collective-permute-done | bytes 262176 | tf_op jit(solution)/shard_map/ppermute | solution.py:102
  44.8 3.7 %collective-permute-start.19 = (bf16[256,256]{1,0:T(8,128)(2,1)S(1)}, bf16[256,256]{1,0:T(8,128)(2,1)S(1)}, u32[]{:S(2)}, u32[]{:S(2)}) collective-permute-start(bf16[256,256]{1,0:T(8,128)(2,1)S(1)} %fusion.45), channel_id=1, source_target_pairs={{0,6},{1,7},{2,4},{3,5},{4,2},{5,3},{6,0},{7,1},{8,14},{9,15},{10,... | collective-permute-start | bytes 393224 | tf_op jit(solution)/shard_map/ppermute | solution.py:102
  50.9 1.2 %collective-permute-start.23 = (bf16[256,256]{1,0:T(8,128)(2,1)S(1)}, bf16[256,256]{1,0:T(8,128)(2,1)S(1)}, u32[]{:S(2)}, u32[]{:S(2)}) collective-permute-start(bf16[256,256]{1,0:T(8,128)(2,1)S(1)} %collective-permute-done.17), channel_id=1, source_target_pairs={{0,16},{1,9},{2,18},{3,11},{4,20},{5,13},{6,22},{7,15},{8,24},{9,1... | collective-permute-start | bytes 393224 | tf_op jit(solution)/shard_map/ppermute | solution.py:102
  52.2 7.3 %collective-permute-done.18 = bf16[256,256]{1,0:T(8,128)(2,1)S(1)} collective-permute-done((bf16[256,256]{1,0:T(8,128)(2,1)S(1)}, bf16[256,256]{1,0:T(8,128)(2,1)S(1)}, u32[]{:S(2)}, u32[]{:S(2)}) %collective-permute-start.18) | collective-permute-done | bytes 131104 | tf_op jit(solution)/shard_map/ppermute | solution.py:102
  59.5 1.1 %collective-permute-start.22 = (bf16[256,256]{1,0:T(8,128)(2,1)S(1)}, bf16[256,256]{1,0:T(8,128)(2,1)S(1)}, u32[]{:S(2)}, u32[]{:S(2)}) collective-permute-start(bf16[256,256]{1,0:T(8,128)(2,1)S(1)} %collective-permute-done.20), channel_id=1, source_target_pairs={{0,8},{1,17},{2,10},{3,19},{4,12},{5,21},{6,14},{7,23},{8,0},{9,25... | collective-permute-start | bytes 393224 | tf_op jit(solution)/shard_map/ppermute | solution.py:102
  62.4 1.8 %collective-permute-start.26 = (bf16[256,256]{1,0:T(8,128)(2,1)S(1)}, bf16[256,256]{1,0:T(8,128)(2,1)S(1)}, u32[]{:S(2)}, u32[]{:S(2)}) collective-permute-start(bf16[256,256]{1,0:T(8,128)(2,1)S(1)} %collective-permute-done.18), channel_id=1, source_target_pairs={{0,16},{1,9},{2,18},{3,11},{4,20},{5,13},{6,22},{7,15},{8,24},{9,1... | collective-permute-start | bytes 393224 | tf_op jit(solution)/shard_map/ppermute | solution.py:102
  65.0 1.2 %collective-permute-start.30 = (bf16[256,256]{1,0:T(8,128)(2,1)S(1)}, bf16[256,256]{1,0:T(8,128)(2,1)S(1)}, u32[]{:S(2)}, u32[]{:S(2)}) collective-permute-start(bf16[256,256]{1,0:T(8,128)(2,1)S(1)} %collective-permute-done.19), channel_id=1, source_target_pairs={{0,8},{1,17},{2,10},{3,19},{4,12},{5,21},{6,14},{7,23},{8,0},{9,25... | collective-permute-start | bytes 393224 | tf_op jit(solution)/shard_map/ppermute | solution.py:102
  69.4 1.4 %collective-permute-start.28 = (bf16[256,256]{1,0:T(8,128)(2,1)S(1)}, bf16[256,256]{1,0:T(8,128)(2,1)S(1)}, u32[]{:S(2)}, u32[]{:S(2)}) collective-permute-start(bf16[256,256]{1,0:T(8,128)(2,1)S(1)} %collective-permute-done.26), channel_id=1, source_target_pairs={{0,8},{1,17},{2,10},{3,19},{4,12},{5,21},{6,14},{7,23},{8,0},{9,25... | collective-permute-start | bytes 393224 | tf_op jit(solution)/shard_map/ppermute | solution.py:102
  71.1 1.7 %collective-permute-done.29 = bf16[256,256]{1,0:T(8,128)(2,1)S(1)} collective-permute-done((bf16[256,256]{1,0:T(8,128)(2,1)S(1)}, bf16[256,256]{1,0:T(8,128)(2,1)S(1)}, u32[]{:S(2)}, u32[]{:S(2)}) %collective-permute-start.29) | collective-permute-done | bytes 131104 | tf_op jit(solution)/shard_map/ppermute | solution.py:102
  73.0 1.1 %collective-permute-start.31 = (bf16[256,256]{1,0:T(8,128)(2,1)S(1)}, bf16[256,256]{1,0:T(8,128)(2,1)S(1)}, u32[]{:S(2)}, u32[]{:S(2)}) collective-permute-start(bf16[256,256]{1,0:T(8,128)(2,1)S(1)} %collective-permute-done.29), channel_id=1, source_target_pairs={{0,8},{1,17},{2,10},{3,19},{4,12},{5,21},{6,14},{7,23},{8,0},{9,25... | collective-permute-start | bytes 393224 | tf_op jit(solution)/shard_map/ppermute | solution.py:102
  75.6 2.5 %collective-permute-done.31 = bf16[256,256]{1,0:T(8,128)(2,1)S(1)} collective-permute-done((bf16[256,256]{1,0:T(8,128)(2,1)S(1)}, bf16[256,256]{1,0:T(8,128)(2,1)S(1)}, u32[]{:S(2)}, u32[]{:S(2)}) %collective-permute-start.31) | collective-permute-done | bytes 131104 | tf_op jit(solution)/shard_map/ppermute | solution.py:102
  (119 shorter events, 24.9 us)
Async XLA Ops:
  0.0 18.6 %collective-permute-start = (bf16[256,256]{1,0:T(8,128)(2,1)}, bf16[256,256]{1,0:T(8,128)(2,1)S(1)}, u32[]{:S(2)}, u32[]{:S(2)}) collective-permute-start(bf16[256,256]{1,0:T(8,128)(2,1)} %param.5), channel_id=1, source_target_pairs={{0,2},{1,3},{2,0},{3,1},{4,6},{5,7},{6,4},{7,5},{8,10},{9,11},{10,... | collective-permute-start | bytes 393224 | tf_op jit(solution)/shard_map/ppermute | solution.py:102
  3.0 15.9 %collective-permute-start.4 = (bf16[256,256]{1,0:T(8,128)(2,1)}, bf16[256,256]{1,0:T(8,128)(2,1)S(1)}, u32[]{:S(2)}, u32[]{:S(2)}) collective-permute-start(bf16[256,256]{1,0:T(8,128)(2,1)} %param.5), channel_id=1, source_target_pairs={{0,8},{1,17},{2,10},{3,19},{4,12},{5,21},{6,14},{7,23},{8,0},{9,25... | collective-permute-start | bytes 393224 | tf_op jit(solution)/shard_map/ppermute | solution.py:102
  4.5 14.6 %collective-permute-start.3 = (bf16[256,256]{1,0:T(8,128)(2,1)}, bf16[256,256]{1,0:T(8,128)(2,1)S(1)}, u32[]{:S(2)}, u32[]{:S(2)}) collective-permute-start(bf16[256,256]{1,0:T(8,128)(2,1)} %param.5), channel_id=1, source_target_pairs={{0,16},{1,9},{2,18},{3,11},{4,20},{5,13},{6,22},{7,15},{8,24},{9,1... | collective-permute-start | bytes 393224 | tf_op jit(solution)/shard_map/ppermute | solution.py:102
  6.0 13.4 %collective-permute-start.2 = (bf16[256,256]{1,0:T(8,128)(2,1)}, bf16[256,256]{1,0:T(8,128)(2,1)S(1)}, u32[]{:S(2)}, u32[]{:S(2)}) collective-permute-start(bf16[256,256]{1,0:T(8,128)(2,1)} %param.5), channel_id=1, source_target_pairs={{0,6},{1,7},{2,4},{3,5},{4,2},{5,3},{6,0},{7,1},{8,14},{9,15},{10,... | collective-permute-start | bytes 393224 | tf_op jit(solution)/shard_map/ppermute | solution.py:102
  8.5 13.0 %collective-permute-start.1 = (bf16[256,256]{1,0:T(8,128)(2,1)}, bf16[256,256]{1,0:T(8,128)(2,1)S(1)}, u32[]{:S(2)}, u32[]{:S(2)}) collective-permute-start(bf16[256,256]{1,0:T(8,128)(2,1)} %param.5), channel_id=1, source_target_pairs={{0,4},{1,5},{2,6},{3,7},{4,0},{5,1},{6,2},{7,3},{8,12},{9,13},{10,... | collective-permute-start | bytes 393224 | tf_op jit(solution)/shard_map/ppermute | solution.py:102
  18.6 19.4 %collective-permute-start.15 = (bf16[16,256,256]{2,1,0:T(8,128)(2,1)}, bf16[16,256,256]{2,1,0:T(8,128)(2,1)S(1)}, u32[]{:S(2)}, u32[]{:S(2)}) collective-permute-start(bf16[16,256,256]{2,1,0:T(8,128)(2,1)} %copy-done.1), channel_id=1, source_target_pairs={{0,1},{1,0},{2,3},{3,2},{4,5},{5,4},{6,7},{7,6},{8,9},{9,8},{10,11... | collective-permute-start | bytes 6291464 | tf_op jit(solution)/shard_map/ppermute | solution.py:102
  18.9 6.2 %collective-permute-start.7 = (bf16[256,256]{1,0:T(8,128)(2,1)S(1)}, bf16[256,256]{1,0:T(8,128)(2,1)S(1)}, u32[]{:S(2)}, u32[]{:S(2)}) collective-permute-start(bf16[256,256]{1,0:T(8,128)(2,1)S(1)} %collective-permute-done), channel_id=1, source_target_pairs={{0,8},{1,17},{2,10},{3,19},{4,12},{5,21},{6,14},{7,23},{8,0},{9,25... | collective-permute-start | bytes 393224 | tf_op jit(solution)/shard_map/ppermute | solution.py:102
  19.2 6.4 %collective-permute-start.6 = (bf16[256,256]{1,0:T(8,128)(2,1)S(1)}, bf16[256,256]{1,0:T(8,128)(2,1)S(1)}, u32[]{:S(2)}, u32[]{:S(2)}) collective-permute-start(bf16[256,256]{1,0:T(8,128)(2,1)S(1)} %collective-permute-done), channel_id=1, source_target_pairs={{0,16},{1,9},{2,18},{3,11},{4,20},{5,13},{6,22},{7,15},{8,24},{9,1... | collective-permute-start | bytes 393224 | tf_op jit(solution)/shard_map/ppermute | solution.py:102
  19.5 18.4 %collective-permute-start.5 = (bf16[256,256]{1,0:T(8,128)(2,1)S(1)}, bf16[256,256]{1,0:T(8,128)(2,1)S(1)}, u32[]{:S(2)}, u32[]{:S(2)}) collective-permute-start(bf16[256,256]{1,0:T(8,128)(2,1)S(1)} %collective-permute-done.3), channel_id=1, source_target_pairs={{0,8},{1,17},{2,10},{3,19},{4,12},{5,21},{6,14},{7,23},{8,0},{9,25... | collective-permute-start | bytes 393224 | tf_op jit(solution)/shard_map/ppermute | solution.py:102
  21.5 7.4 %collective-permute-start.10 = (bf16[256,256]{1,0:T(8,128)(2,1)S(1)}, bf16[256,256]{1,0:T(8,128)(2,1)S(1)}, u32[]{:S(2)}, u32[]{:S(2)}) collective-permute-start(bf16[256,256]{1,0:T(8,128)(2,1)S(1)} %collective-permute-done.1), channel_id=1, source_target_pairs={{0,8},{1,17},{2,10},{3,19},{4,12},{5,21},{6,14},{7,23},{8,0},{9,25... | collective-permute-start | bytes 393224 | tf_op jit(solution)/shard_map/ppermute | solution.py:102
  25.6 10.0 %collective-permute-start.13 = (bf16[256,256]{1,0:T(8,128)(2,1)S(1)}, bf16[256,256]{1,0:T(8,128)(2,1)S(1)}, u32[]{:S(2)}, u32[]{:S(2)}) collective-permute-start(bf16[256,256]{1,0:T(8,128)(2,1)S(1)} %collective-permute-done.2), channel_id=1, source_target_pairs={{0,8},{1,17},{2,10},{3,19},{4,12},{5,21},{6,14},{7,23},{8,0},{9,25... | collective-permute-start | bytes 393224 | tf_op jit(solution)/shard_map/ppermute | solution.py:102
  29.0 6.4 %collective-permute-start.12 = (bf16[256,256]{1,0:T(8,128)(2,1)S(1)}, bf16[256,256]{1,0:T(8,128)(2,1)S(1)}, u32[]{:S(2)}, u32[]{:S(2)}) collective-permute-start(bf16[256,256]{1,0:T(8,128)(2,1)S(1)} %collective-permute-done.2), channel_id=1, source_target_pairs={{0,16},{1,9},{2,18},{3,11},{4,20},{5,13},{6,22},{7,15},{8,24},{9,1... | collective-permute-start | bytes 393224 | tf_op jit(solution)/shard_map/ppermute | solution.py:102
  30.5 9.9 %collective-permute-start.8 = (bf16[256,256]{1,0:T(8,128)(2,1)S(1)}, bf16[256,256]{1,0:T(8,128)(2,1)S(1)}, u32[]{:S(2)}, u32[]{:S(2)}) collective-permute-start(bf16[256,256]{1,0:T(8,128)(2,1)S(1)} %collective-permute-done.6), channel_id=1, source_target_pairs={{0,8},{1,17},{2,10},{3,19},{4,12},{5,21},{6,14},{7,23},{8,0},{9,25... | collective-permute-start | bytes 393224 | tf_op jit(solution)/shard_map/ppermute | solution.py:102
  35.5 6.2 %collective-permute-start.14 = (bf16[256,256]{1,0:T(8,128)(2,1)S(1)}, bf16[256,256]{1,0:T(8,128)(2,1)S(1)}, u32[]{:S(2)}, u32[]{:S(2)}) collective-permute-start(bf16[256,256]{1,0:T(8,128)(2,1)S(1)} %collective-permute-done.12), channel_id=1, source_target_pairs={{0,8},{1,17},{2,10},{3,19},{4,12},{5,21},{6,14},{7,23},{8,0},{9,25... | collective-permute-start | bytes 393224 | tf_op jit(solution)/shard_map/ppermute | solution.py:102
  43.8 18.6 %collective-permute-start.21 = (bf16[256,256]{1,0:T(8,128)(2,1)S(1)}, bf16[256,256]{1,0:T(8,128)(2,1)S(1)}, u32[]{:S(2)}, u32[]{:S(2)}) collective-permute-start(bf16[256,256]{1,0:T(8,128)(2,1)S(1)} %fusion.45), channel_id=1, source_target_pairs={{0,8},{1,17},{2,10},{3,19},{4,12},{5,21},{6,14},{7,23},{8,0},{9,25... | collective-permute-start | bytes 393224 | tf_op jit(solution)/shard_map/ppermute | solution.py:102
  44.8 16.0 %collective-permute-start.19 = (bf16[256,256]{1,0:T(8,128)(2,1)S(1)}, bf16[256,256]{1,0:T(8,128)(2,1)S(1)}, u32[]{:S(2)}, u32[]{:S(2)}) collective-permute-start(bf16[256,256]{1,0:T(8,128)(2,1)S(1)} %fusion.45), channel_id=1, source_target_pairs={{0,6},{1,7},{2,4},{3,5},{4,2},{5,3},{6,0},{7,1},{8,14},{9,15},{10,... | collective-permute-start | bytes 393224 | tf_op jit(solution)/shard_map/ppermute | solution.py:102
  48.6 11.0 %collective-permute-start.18 = (bf16[256,256]{1,0:T(8,128)(2,1)S(1)}, bf16[256,256]{1,0:T(8,128)(2,1)S(1)}, u32[]{:S(2)}, u32[]{:S(2)}) collective-permute-start(bf16[256,256]{1,0:T(8,128)(2,1)S(1)} %fusion.45), channel_id=1, source_target_pairs={{0,4},{1,5},{2,6},{3,7},{4,0},{5,1},{6,2},{7,3},{8,12},{9,13},{10,... | collective-permute-start | bytes 393224 | tf_op jit(solution)/shard_map/ppermute | solution.py:102
  49.8 16.8 %collective-permute-start.24 = (bf16[256,256]{1,0:T(8,128)(2,1)S(1)}, bf16[256,256]{1,0:T(8,128)(2,1)S(1)}, u32[]{:S(2)}, u32[]{:S(2)}) collective-permute-start(bf16[256,256]{1,0:T(8,128)(2,1)S(1)} %collective-permute-done.17), channel_id=1, source_target_pairs={{0,8},{1,17},{2,10},{3,19},{4,12},{5,21},{6,14},{7,23},{8,0},{9,25... | collective-permute-start | bytes 393224 | tf_op jit(solution)/shard_map/ppermute | solution.py:102
  50.9 14.2 %collective-permute-start.23 = (bf16[256,256]{1,0:T(8,128)(2,1)S(1)}, bf16[256,256]{1,0:T(8,128)(2,1)S(1)}, u32[]{:S(2)}, u32[]{:S(2)}) collective-permute-start(bf16[256,256]{1,0:T(8,128)(2,1)S(1)} %collective-permute-done.17), channel_id=1, source_target_pairs={{0,16},{1,9},{2,18},{3,11},{4,20},{5,13},{6,22},{7,15},{8,24},{9,1... | collective-permute-start | bytes 393224 | tf_op jit(solution)/shard_map/ppermute | solution.py:102
  59.5 15.0 %collective-permute-start.22 = (bf16[256,256]{1,0:T(8,128)(2,1)S(1)}, bf16[256,256]{1,0:T(8,128)(2,1)S(1)}, u32[]{:S(2)}, u32[]{:S(2)}) collective-permute-start(bf16[256,256]{1,0:T(8,128)(2,1)S(1)} %collective-permute-done.20), channel_id=1, source_target_pairs={{0,8},{1,17},{2,10},{3,19},{4,12},{5,21},{6,14},{7,23},{8,0},{9,25... | collective-permute-start | bytes 393224 | tf_op jit(solution)/shard_map/ppermute | solution.py:102
  60.9 8.5 %collective-permute-start.27 = (bf16[256,256]{1,0:T(8,128)(2,1)S(1)}, bf16[256,256]{1,0:T(8,128)(2,1)S(1)}, u32[]{:S(2)}, u32[]{:S(2)}) collective-permute-start(bf16[256,256]{1,0:T(8,128)(2,1)S(1)} %collective-permute-done.18), channel_id=1, source_target_pairs={{0,8},{1,17},{2,10},{3,19},{4,12},{5,21},{6,14},{7,23},{8,0},{9,25... | collective-permute-start | bytes 393224 | tf_op jit(solution)/shard_map/ppermute | solution.py:102
  65.0 9.3 %collective-permute-start.30 = (bf16[256,256]{1,0:T(8,128)(2,1)S(1)}, bf16[256,256]{1,0:T(8,128)(2,1)S(1)}, u32[]{:S(2)}, u32[]{:S(2)}) collective-permute-start(bf16[256,256]{1,0:T(8,128)(2,1)S(1)} %collective-permute-done.19), channel_id=1, source_target_pairs={{0,8},{1,17},{2,10},{3,19},{4,12},{5,21},{6,14},{7,23},{8,0},{9,25... | collective-permute-start | bytes 393224 | tf_op jit(solution)/shard_map/ppermute | solution.py:102
  66.6 6.2 %collective-permute-start.29 = (bf16[256,256]{1,0:T(8,128)(2,1)S(1)}, bf16[256,256]{1,0:T(8,128)(2,1)S(1)}, u32[]{:S(2)}, u32[]{:S(2)}) collective-permute-start(bf16[256,256]{1,0:T(8,128)(2,1)S(1)} %collective-permute-done.19), channel_id=1, source_target_pairs={{0,16},{1,9},{2,18},{3,11},{4,20},{5,13},{6,22},{7,15},{8,24},{9,1... | collective-permute-start | bytes 393224 | tf_op jit(solution)/shard_map/ppermute | solution.py:102
  68.3 6.9 %collective-permute-start.25 = (bf16[256,256]{1,0:T(8,128)(2,1)S(1)}, bf16[256,256]{1,0:T(8,128)(2,1)S(1)}, u32[]{:S(2)}, u32[]{:S(2)}) collective-permute-start(bf16[256,256]{1,0:T(8,128)(2,1)S(1)} %collective-permute-done.23), channel_id=1, source_target_pairs={{0,8},{1,17},{2,10},{3,19},{4,12},{5,21},{6,14},{7,23},{8,0},{9,25... | collective-permute-start | bytes 393224 | tf_op jit(solution)/shard_map/ppermute | solution.py:102
  (13 other events, 58.3 us)

commit v2 on v1

v2 whole, which is shorter than its diff:
```python
import functools
import math

import jax
import jax.numpy as jnp
from jax import lax
from jax.experimental import pallas as pl
from jax.experimental.pallas import tpu as pltpu
from jax.sharding import PartitionSpec as P

HOPS = 2
VLIM = 48 << 20
AXES = ("blk", "rep")
LONG = pl.CostEstimate(flops=0, bytes_accessed=1 << 32, transcendentals=0)


def piece_lanes(panel, member, side, members, rows_dev):
    flat = jnp.arange(side * side * members, dtype=jnp.int32)
    panels, sources = flat // members, flat % members
    down = (panel // side - panels // side + side) % side
    across = (panel % side - panels % side + side) % side
    first = jnp.where(sources % 2 == 0, down, across)
    second = jnp.where(sources % 2 == 0, across, down)
    apart = (member // 2) ^ (sources // 2)
    run = jnp.where(first > 0, apart, apart - 1)
    slot = jnp.where(first > 0, first - 1, side - 1)
    length = jnp.where(run < members // 2 - 1, side, side - 1)
    return jnp.where(run < 0, second, side + run * side * side + length * second + slot) * rows_dev


def expand_kernel(lanes_of, cols, counts, core, tiles, *refs, members, counting):
    if counting:
        wanted, dense, restart, token, sem = refs
        token[...] = jnp.zeros_like(token)
    else:
        _, dense, sem = refs
    blocks_dev, panels, _, bs, _ = tiles.shape
    dense[...] = jnp.zeros_like(dense)
    mine = core[0]

    started = jnp.int32(0)
    for i in range(blocks_dev):
        for p in range(panels):

            def step(k, started, i=i, p=p):
                block = cols[i, p, k]
                source = block // blocks_dev
                here = source % 2 == mine

                @pl.when(here)
                def _():
                    lane = pl.multiple_of(lanes_of[p * members + source] + block % blocks_dev * bs, bs)
                    target = dense.at[pl.ds(i * bs, bs), pl.ds(lane, bs)]
                    pltpu.make_async_copy(tiles.at[i, p, k], target, sem).start()

                return started + here.astype(jnp.int32)

            started = lax.fori_loop(0, counts[i, p], step, started)

    if counting:
        node = core[1] + lax.broadcasted_iota(jnp.int32, restart.shape, 0)
        total = jnp.zeros(restart.shape, jnp.float32)
        for j in range(wanted.shape[0]):
            total += (node == wanted[j : j + 1, :]).astype(jnp.float32)
        restart[...] = total

    def arrive(_, carry):
        pltpu.make_async_copy(tiles.at[0, 0, 0], dense.at[pl.ds(0, bs), pl.ds(0, bs)], sem).wait()
        return carry

    lax.fori_loop(0, started, arrive, 0)


def expand(lanes_of, cols, counts, core, tiles, members, wanted=None, token=None):
    blocks_dev, panels, slots, bs, _ = tiles.shape
    rows = blocks_dev * bs
    columns = lanes_of.shape[0] // 2 * rows
    smem, vmem = pl.BlockSpec(memory_space=pltpu.SMEM), pl.BlockSpec(memory_space=pltpu.VMEM)
    counting = wanted is not None
    out_shape = [jax.ShapeDtypeStruct((rows, columns), tiles.dtype)]
    if counting:
        out_shape.append(jax.ShapeDtypeStruct((rows, wanted.shape[1]), jnp.float32))
        out_shape.append(jax.ShapeDtypeStruct((8, 128), jnp.float32))
    return pl.pallas_call(
        functools.partial(expand_kernel, members=members, counting=counting),
        out_shape=out_shape,
        in_specs=[smem] * 4
        + [pl.BlockSpec(memory_space=pltpu.HBM), vmem if counting else pl.BlockSpec(memory_space=pl.ANY)],
        out_specs=[vmem] * len(out_shape),
        scratch_shapes=[pltpu.SemaphoreType.DMA],
        compiler_params=pltpu.CompilerParams(vmem_limit_bytes=VLIM),
        cost_estimate=LONG,
        name="expand_blocks",
    )(lanes_of, cols, counts, core, tiles, wanted if counting else token)


def pause(value):
    anywhere = pl.BlockSpec(memory_space=pl.ANY)
    return pl.pallas_call(
        lambda given, passed: None,
        out_shape=jax.ShapeDtypeStruct(value.shape, value.dtype),
        in_specs=[anywhere],
        out_specs=anywhere,
        input_output_aliases={0: 0},
        cost_estimate=LONG,
        name="pause",
    )(value)


def multiply_kernel(theirs, mine, *refs, places, added):
    *values, total = refs
    given = values.pop() if added else None
    rows = mine.shape[0]
    for half, weights in enumerate((theirs, mine)):
        at = pl.ds(half * rows, rows)
        done = given[at, :] if added else None
        for place, value in zip(places, values, strict=True):
            product = jnp.dot(
                weights[:, place : place + value.shape[0]], value[...], preferred_element_type=jnp.float32
            )
            done = product if done is None else done + product
        total[at, :] = done


def multiply(halves, items, total=None):
    places, values = zip(*items, strict=True)
    vmem = pl.BlockSpec(memory_space=pltpu.VMEM)
    given = [] if total is None else [total]
    return pl.pallas_call(
        functools.partial(multiply_kernel, places=places, added=bool(given)),
        out_shape=jax.ShapeDtypeStruct((2 * halves[1].shape[0], values[0].shape[1]), jnp.float32),
        in_specs=[vmem] * (2 + len(values) + len(given)),
        out_specs=vmem,
        input_output_aliases={2 + len(values): 0} if given else {},
        compiler_params=pltpu.CompilerParams(vmem_limit_bytes=(8 << 20) + 4 * halves[1].size),
        cost_estimate=LONG,
        name="multiply_pieces",
    )(*halves, *values, *given)


def permutes(side, depth):
    places = [
        (y, x, z, c) for y in range(side) for x in range(side) for z in range(depth) for c in range(2)
    ]

    def index(y, x, z, c):
        return (((y % side) * side + x % side) * depth + z) * 2 + c

    def pairs(move):
        return [(index(*place), index(*move(*place))) for place in places]

    along = {k: pairs(lambda y, x, z, c: (y, x, z ^ k, c)) for k in range(1, depth)}
    first = {
        j: pairs(lambda y, x, z, c: (y, x + j, z, c) if c else (y + j, x, z, c)) for j in range(1, side)
    }
    second = {
        j: pairs(lambda y, x, z, c: (y + j, x, z, c) if c else (y, x + j, z, c)) for j in range(1, side)
    }
    return along, first, second, pairs(lambda y, x, z, c: (y, x, z, 1 - c))


def per_device(scores, tiles, cols, counts, seeds):
    rows_dev = scores.shape[0]
    members = lax.axis_size("rep")
    side = math.isqrt(lax.axis_size("blk"))
    depth = members // 2
    panel = lax.axis_index("blk")
    member = lax.axis_index("rep")
    lanes_of = piece_lanes(panel, member, side, members, rows_dev).astype(jnp.int32)
    core = jnp.stack([member % 2, (panel * members + member) * rows_dev]).astype(jnp.int32)
    along, first, second, across = permutes(side, depth)

    def send(value, pairs):
        return lax.ppermute(value, AXES, pairs)

    def joined(values):
        return values[0] if len(values) == 1 else jnp.concatenate(values, axis=0)

    def after(value, *others):
        return lax.optimization_barrier((value, *others))[0]

    steps = range(1, side)
    runs = [side + d * side * side for d in range(depth)]
    others = send(cols, across), send(counts, across), send(tiles, across)

    def lane(place):
        return place * rows_dev

    def stepped(run, length, values):
        return [(lane(run + b * length), value) for b, value in zip(steps, values, strict=True)]

    current = scores
    for hop_index in range(HOPS):
        o = current
        q = send(o, along[2])
        f0 = joined([send(o, first[a]) for a in steps])
        p = send(o, along[1])
        s0 = [send(o, second[b]) for b in steps]
        if hop_index:
            total = multiply(both, [(lane(0), o)])
            q = after(q, total)
        else:
            half, restart, token = expand(lanes_of, cols, counts, core, tiles, members, seeds.T)
            q = after(q, half)
        f2 = joined([send(q, first[a]) for a in steps])
        m0 = joined([f0, p])
        early = [(lane(runs[1] + side - 1), q), (lane(runs[0]), m0)]
        if hop_index:
            anchor = total = multiply(both, early, total)
        else:
            anchor = token = pause(after(token, q, f0, p, *others))
        f2 = after(f2, anchor)
        r = send(after(q, anchor), along[1])
        f1 = send(after(f0, anchor), along[1])
        t0 = [send(after(m0, anchor), second[b]) for b in steps]
        f3 = send(f2, along[1])
        m1, m2 = joined([after(f1, f2), q]), joined([f2, r])
        t1 = [send(m1, second[b]) for b in steps]
        t2 = [send(m2, second[b]) for b in steps]
        later = stepped(runs[0], side, t0) + [(lane(b), s) for b, s in zip(steps, s0)] + [(lane(runs[2]), f2)]
        if hop_index:
            anchor = total = multiply(both, later, total)
        else:
            given = after(lanes_of, f2, *t0, *s0)
            both = [*expand(given, others[0], others[1], core, others[2], members, token=token), half]
            anchor = both[0]
            later = [(lane(0), o), *early, *later]
        f3 = after(f3, anchor)
        t3 = [send(f3, second[b]) for b in steps]
        items = [(lane(runs[1]), f1), (lane(runs[2] + side - 1), r), (lane(runs[3]), f3)]
        items += stepped(runs[1], side, t1) + stepped(runs[2], side, t2)
        total = multiply(both, items, total) if hop_index else multiply(both, later + items)
        theirs, mine = total[:rows_dev], total[rows_dev:]
        for start, value in stepped(runs[3], side - 1, t3):
            at = slice(start, start + value.shape[0])
            theirs += jnp.dot(both[0][:, at], value, preferred_element_type=jnp.float32)
            mine += jnp.dot(both[1][:, at], value, preferred_element_type=jnp.float32)
        summed = mine + send(theirs, across)
        current = (0.9 * summed + restart).astype(jnp.bfloat16)
    return current


def solution(mesh):
    return jax.shard_map(
        per_device,
        mesh=mesh,
        in_specs=(
            P(AXES, None),
            P(AXES, None, None, None, None),
            P(AXES, None, None),
            P(AXES, None),
            P(),
        ),
        out_specs=P(AXES, None),
        check_vma=False,
    )
```

time: 81 us -> 67.3 us (0.83)
  matrix products: 12.5 us -> 0.73 us
  starting transfers between devices: 32.6 us -> 27.7 us
  Pallas kernels: 5.34 us -> 8.29 us
    dot_general x64 -> x4, matrix products: 12.5 us -> 0.73 us  [the longest x2 0.37 us: per_device(): theirs += jnp.dot(both[0][:, at], value, preferred_element_type=jnp.float32)]
    ppermute x33 -> x29, starting transfers between devices: 32.6 us -> 27.7 us  [send(): return lax.ppermute(value, AXES, pairs)]
    pallas_call x1 -> x8, Pallas kernels: 5.34 us -> 8.29 us  [the longest x2 5.4 us: expand(): pl.pallas_call(functools.partial(expand_kernel, members=members, counting...]
    reduce_sum x1 -> x0, other arithmetic: 1.52 us -> none  [per_device(): jnp.sum((node_ids[:, None, None] == seeds[None, :, :]).astype(jnp.float32...]
    unnamed x8 -> x14, local copies, waits for them, and re-layouts: 2.03 us -> 3.37 us
    ppermute x33 -> x29, waiting for transfers between devices: 25.1 us -> 25.5 us  [send(): return lax.ppermute(value, AXES, pairs)]
  transfers between devices with their start and end apart: 33 -> 29, of which waited for: 13 -> 17; matrix products, arithmetic and copies ran while one was open for 17% -> 1% of each run, Pallas kernels for 7% -> 12%
where the time goes in v2:
time: 67.3 us; the launch traced here: 66.8 us
  starting transfers between devices  27.7 us (41%)
  waiting for transfers between devices  25.5 us (38%)
  Pallas kernels  8.29 us (12%)
  local copies, waits for them, and re-layouts  3.39 us (5%)
  other arithmetic  0.97 us (1%)
  matrix products  0.73 us (1%)
    ppermute x29, starting transfers between devices, send(): return lax.ppermute(value, AXES, pairs)  27.7 us
    ppermute x29, waiting for transfers between devices, send(): return lax.ppermute(value, AXES, pairs)  25.5 us
    pallas_call x2, Pallas kernels, expand(): pl.pallas_call(functools.partial(expand_kernel, members=members, counting...  5.4 us
    unnamed x14, local copies, waits for them, and re-layouts  3.37 us
    pallas_call x5, Pallas kernels, multiply(): pl.pallas_call(functools.partial(multiply_kernel, places=places, added=bo...  2.88 us
  transfers between devices with their start and end apart: 29, of which 17 were waited for; matrix products, arithmetic and copies ran while one was open for 1% of the time, Pallas kernels for 12%

profile of v2, /device:TPU:0, one launch (start us, length us, event | category | flops | bytes accessed | tf_op | source)
XLA Modules:
  0.0 66.8 jit_solution(4521693160908400663)
XLA Ops:
  0.5 3.6 %collective-permute-start = (bf16[256,256]{1,0:T(8,128)(2,1)}, bf16[256,256]{1,0:T(8,128)(2,1)S(1)}, u32[]{:S(2)}, u32[]{:S(2)}) collective-permute-start(bf16[256,256]{1,0:T(8,128)(2,1)} %refs_0_.1), channel_id=1, source_target_pairs={{0,4},{1,5},{2,6},{3,7},{4,0},{5,1},{6,2},{7,3},{8,12},{9,13},{10,... | collective-permute-start | bytes 393224 | tf_op jit(solution)/shard_map/ppermute | solution.py:174
  4.0 1.5 %collective-permute-start.2 = (bf16[256,256]{1,0:T(8,128)(2,1)}, bf16[256,256]{1,0:T(8,128)(2,1)S(1)}, u32[]{:S(2)}, u32[]{:S(2)}) collective-permute-start(bf16[256,256]{1,0:T(8,128)(2,1)} %refs_0_.1), channel_id=1, source_target_pairs={{0,16},{1,9},{2,18},{3,11},{4,20},{5,13},{6,22},{7,15},{8,24},{9,1... | collective-permute-start | bytes 393224 | tf_op jit(solution)/shard_map/ppermute | solution.py:174
  5.6 1.6 %collective-permute-start.3 = (bf16[256,256]{1,0:T(8,128)(2,1)}, bf16[256,256]{1,0:T(8,128)(2,1)S(1)}, u32[]{:S(2)}, u32[]{:S(2)}) collective-permute-start(bf16[256,256]{1,0:T(8,128)(2,1)} %refs_0_.1), channel_id=1, source_target_pairs={{0,2},{1,3},{2,0},{3,1},{4,6},{5,7},{6,4},{7,5},{8,10},{9,11},{10,... | collective-permute-start | bytes 393224 | tf_op jit(solution)/shard_map/ppermute | solution.py:174
  9.3 3.4 %expand_blocks.2 = (bf16[256,4096]{1,0:T(8,128)(2,1)S(1)}, f32[256,256]{1,0:T(8,128)S(1)}, f32[8,128]{1,0:T(8,128)S(1)}) custom-call(s32[32]{0:T(128)S(1)} %fusion.27.lanes_of, s32[2,4,16]{2,1,0:T(4,128)S(1)} %copy-done.4, s32[2,4]{1,0:T(2,128)S(1)} %copy-done.5, s32[2]{0:T(128)S(1)} %pad_add_fusion.core, bf16[2,4,16,128,128]{4,3,2,1,0:T(8,128)(2,1)} %tiles.1, ...), custom_call_target="tpu_custom_call" | custom-call | bytes 4294967296 | tf_op jit(solution)/shard_map/expand_blocks/pallas_call | solution.py:84
  13.3 1.1 %collective-permute-done.5.counts = s32[2,4]{1,0:T(2,128)S(1)} collective-permute-done((s32[2,4]{1,0:T(2,128)S(1)}, s32[2,4]{1,0:T(2,128)S(1)}, u32[]{:S(2)}, u32[]{:S(2)}) %collective-permute-start.5) | collective-permute-done | bytes 64 | tf_op jit(solution)/shard_map/ppermute | solution.py:174
  16.3 1.4 %collective-permute-start.10 = (bf16[256,256]{1,0:T(8,128)(2,1)S(1)}, bf16[256,256]{1,0:T(8,128)(2,1)S(1)}, u32[]{:S(2)}, u32[]{:S(2)}) collective-permute-start(bf16[256,256]{1,0:T(8,128)(2,1)S(1)} %collective-permute-done.refs_1_), channel_id=1, source_target_pairs={{0,2},{1,3},{2,0},{3,1},{4,6},{5,7},{6,4},{7,5},{8,10},{9,11},{10,... | collective-permute-start | bytes 393224 | tf_op jit(solution)/shard_map/ppermute | solution.py:174
  17.8 2.3 %collective-permute-done.1.refs_5_ = bf16[256,256]{1,0:T(8,128)(2,1)S(1)} collective-permute-done((bf16[256,256]{1,0:T(8,128)(2,1)S(1)}, bf16[256,256]{1,0:T(8,128)(2,1)S(1)}, u32[]{:S(2)}, u32[]{:S(2)}) %collective-permute-start.1) | collective-permute-done | bytes 131104 | tf_op jit(solution)/shard_map/ppermute | solution.py:174
  20.0 1.4 %collective-permute-start.7 = (bf16[512,256]{1,0:T(8,128)(2,1)S(1)}, bf16[512,256]{1,0:T(8,128)(2,1)S(1)}, u32[]{:S(2)}, u32[]{:S(2)}) collective-permute-start(bf16[512,256]{1,0:T(8,128)(2,1)S(1)} %constant_dynamic-update-slice_fusion.refs_2_), channel_id=1, source_target_pairs={{0,8},{1,17},{2,10},{3,19},{4,12},{5,21},{6,14},{7,23},{8,0},{9,25... | collective-permute-start | bytes 786440 | tf_op jit(solution)/shard_map/ppermute | solution.py:174
  23.9 1.6 %collective-permute-start.13 = (bf16[512,256]{1,0:T(8,128)(2,1)S(1)}, bf16[512,256]{1,0:T(8,128)(2,1)S(1)}, u32[]{:S(2)}, u32[]{:S(2)}) collective-permute-start(bf16[512,256]{1,0:T(8,128)(2,1)S(1)} %pad_maximum_fusion.1), channel_id=1, source_target_pairs={{0,8},{1,17},{2,10},{3,19},{4,12},{5,21},{6,14},{7,23},{8,0},{9,25... | collective-permute-start | bytes 786440 | tf_op jit(solution)/shard_map/ppermute | solution.py:174
  27.1 2.0 %expand_blocks.3.theirs = bf16[256,4096]{1,0:T(8,128)(2,1)S(1)} custom-call(s32[32]{0:T(128)S(1)} %fusion.27.lanes_of, s32[2,4,16]{2,1,0:T(4,128)S(1)} %collective-permute-done.4.cols, s32[2,4]{1,0:T(2,128)S(1)} %collective-permute-done.5.counts, s32[2]{0:T(128)S(1)} %pad_add_fusion.core, bf16[2,4,16,128,128]{4,3,2,1,0:T(8,128)(2,1)} %collective-permute-done.6.tiles, ...), custom_call_target="tpu_custom_call" | custom-call | bytes 4294967296 | tf_op jit(solution)/shard_map/expand_blocks/pallas_call | solution.py:84
  29.1 1.5 %collective-permute-start.14 = (bf16[256,256]{1,0:T(8,128)(2,1)S(1)}, bf16[256,256]{1,0:T(8,128)(2,1)S(1)}, u32[]{:S(2)}, u32[]{:S(2)}) collective-permute-start(bf16[256,256]{1,0:T(8,128)(2,1)S(1)} %collective-permute-done.11.refs_8_), channel_id=1, source_target_pairs={{0,8},{1,17},{2,10},{3,19},{4,12},{5,21},{6,14},{7,23},{8,0},{9,25... | collective-permute-start | bytes 393224 | tf_op jit(solution)/shard_map/ppermute | solution.py:174
  30.6 1.4 %collective-permute-done.13.refs_10_ = bf16[512,256]{1,0:T(8,128)(2,1)S(1)} collective-permute-done((bf16[512,256]{1,0:T(8,128)(2,1)S(1)}, bf16[512,256]{1,0:T(8,128)(2,1)S(1)}, u32[]{:S(2)}, u32[]{:S(2)}) %collective-permute-start.13) | collective-permute-done | bytes 262176 | tf_op jit(solution)/shard_map/ppermute | solution.py:174
  32.0 1.2 %multiply_pieces.5 = f32[512,256]{1,0:T(8,128)S(1)} custom-call(bf16[256,4096]{1,0:T(8,128)(2,1)S(1)} %expand_blocks.3.theirs, bf16[256,4096]{1,0:T(8,128)(2,1)S(1)} %get-tuple-element.24.mine, bf16[256,256]{1,0:T(8,128)(2,1)S(1)} %copy-done, bf16[256,256]{1,0:T(8,128)(2,1)S(1)} %collective-permute-done.refs_1_, ...), custom_call_target="tpu_custom_call" | custom-call | bytes 4294967296 | tf_op jit(solution)/shard_map/multiply_pieces/pallas_call | solution.py:129
  34.6 1.3 %collective-permute-done.15 = f32[256,256]{1,0:T(8,128)S(1)} collective-permute-done((f32[256,256]{1,0:T(8,128)S(1)}, f32[256,256]{1,0:T(8,128)S(1)}, u32[]{:S(2)}, u32[]{:S(2)}) %collective-permute-start.15) | collective-permute-done | bytes 262176 | tf_op jit(solution)/shard_map/ppermute | solution.py:174
  37.7 2.8 %collective-permute-start.18 = (bf16[256,256]{1,0:T(8,128)(2,1)S(1)}, bf16[256,256]{1,0:T(8,128)(2,1)S(1)}, u32[]{:S(2)}, u32[]{:S(2)}) collective-permute-start(bf16[256,256]{1,0:T(8,128)(2,1)S(1)} %fusion.7.refs_0_), channel_id=1, source_target_pairs={{0,2},{1,3},{2,0},{3,1},{4,6},{5,7},{6,4},{7,5},{8,10},{9,11},{10,... | collective-permute-start | bytes 393224 | tf_op jit(solution)/shard_map/ppermute | solution.py:174
  40.8 4.7 %collective-permute-done.17.refs_0_ = bf16[256,256]{1,0:T(8,128)(2,1)S(1)} collective-permute-done((bf16[256,256]{1,0:T(8,128)(2,1)S(1)}, bf16[256,256]{1,0:T(8,128)(2,1)S(1)}, u32[]{:S(2)}, u32[]{:S(2)}) %collective-permute-start.17) | collective-permute-done | bytes 131104 | tf_op jit(solution)/shard_map/ppermute | solution.py:174
  45.5 1.2 %collective-permute-start.21 = (bf16[256,256]{1,0:T(8,128)(2,1)S(1)}, bf16[256,256]{1,0:T(8,128)(2,1)S(1)}, u32[]{:S(2)}, u32[]{:S(2)}) collective-permute-start(bf16[256,256]{1,0:T(8,128)(2,1)S(1)} %collective-permute-done.17.refs_0_), channel_id=1, source_target_pairs={{0,16},{1,9},{2,18},{3,11},{4,20},{5,13},{6,22},{7,15},{8,24},{9,1... | collective-permute-start | bytes 393224 | tf_op jit(solution)/shard_map/ppermute | solution.py:174
  47.2 2.0 %collective-permute-start.20 = (bf16[256,256]{1,0:T(8,128)(2,1)S(1)}, bf16[256,256]{1,0:T(8,128)(2,1)S(1)}, u32[]{:S(2)}, u32[]{:S(2)}) collective-permute-start(bf16[256,256]{1,0:T(8,128)(2,1)S(1)} %collective-permute-done.17.refs_0_), channel_id=1, source_target_pairs={{0,2},{1,3},{2,0},{3,1},{4,6},{5,7},{6,4},{7,5},{8,10},{9,11},{10,... | collective-permute-start | bytes 393224 | tf_op jit(solution)/shard_map/ppermute | solution.py:174
  49.5 1.7 %collective-permute-start.23 = (bf16[512,256]{1,0:T(8,128)(2,1)S(1)}, bf16[512,256]{1,0:T(8,128)(2,1)S(1)}, u32[]{:S(2)}, u32[]{:S(2)}) collective-permute-start(bf16[512,256]{1,0:T(8,128)(2,1)S(1)} %constant_dynamic-update-slice_fusion.2.refs_1_), channel_id=1, source_target_pairs={{0,8},{1,17},{2,10},{3,19},{4,12},{5,21},{6,14},{7,23},{8,0},{9,25... | collective-permute-start | bytes 786440 | tf_op jit(solution)/shard_map/ppermute | solution.py:174
  51.3 2.3 %collective-permute-done.19.refs_0_ = bf16[256,256]{1,0:T(8,128)(2,1)S(1)} collective-permute-done((bf16[256,256]{1,0:T(8,128)(2,1)S(1)}, bf16[256,256]{1,0:T(8,128)(2,1)S(1)}, u32[]{:S(2)}, u32[]{:S(2)}) %collective-permute-start.19) | collective-permute-done | bytes 131104 | tf_op jit(solution)/shard_map/ppermute | solution.py:174
  53.9 2.5 %collective-permute-done.20.refs_1_ = bf16[256,256]{1,0:T(8,128)(2,1)S(1)} collective-permute-done((bf16[256,256]{1,0:T(8,128)(2,1)S(1)}, bf16[256,256]{1,0:T(8,128)(2,1)S(1)}, u32[]{:S(2)}, u32[]{:S(2)}) %collective-permute-start.20) | collective-permute-done | bytes 131104 | tf_op jit(solution)/shard_map/ppermute | solution.py:174
  57.9 1.2 %collective-permute-start.27 = (bf16[256,256]{1,0:T(8,128)(2,1)S(1)}, bf16[256,256]{1,0:T(8,128)(2,1)S(1)}, u32[]{:S(2)}, u32[]{:S(2)}) collective-permute-start(bf16[256,256]{1,0:T(8,128)(2,1)S(1)} %collective-permute-done.22.refs_2_), channel_id=1, source_target_pairs={{0,8},{1,17},{2,10},{3,19},{4,12},{5,21},{6,14},{7,23},{8,0},{9,25... | collective-permute-start | bytes 393224 | tf_op jit(solution)/shard_map/ppermute | solution.py:174
  60.1 2.8 %collective-permute-done.26.refs_4_ = bf16[512,256]{1,0:T(8,128)(2,1)S(1)} collective-permute-done((bf16[512,256]{1,0:T(8,128)(2,1)S(1)}, bf16[512,256]{1,0:T(8,128)(2,1)S(1)}, u32[]{:S(2)}, u32[]{:S(2)}) %collective-permute-start.26) | collective-permute-done | bytes 262176 | tf_op jit(solution)/shard_map/ppermute | solution.py:174
  64.7 1.3 %collective-permute-done.28 = f32[256,256]{1,0:T(8,128)S(1)} collective-permute-done((f32[256,256]{1,0:T(8,128)S(1)}, f32[256,256]{1,0:T(8,128)S(1)}, u32[]{:S(2)}, u32[]{:S(2)}) %collective-permute-start.28) | collective-permute-done | bytes 262176 | tf_op jit(solution)/shard_map/ppermute | solution.py:174
  (70 shorter events, 18.7 us)
Async XLA Ops:
  0.0 15.6 %collective-permute-start.6 = (bf16[2,4,16,128,128]{4,3,2,1,0:T(8,128)(2,1)}, bf16[2,4,16,128,128]{4,3,2,1,0:T(8,128)(2,1)}, u32[]{:S(2)}, u32[]{:S(2)}) collective-permute-start(bf16[2,4,16,128,128]{4,3,2,1,0:T(8,128)(2,1)} %tiles.1), channel_id=1, source_target_pairs={{0,1},{1,0},{2,3},{3,2},{4,5},{5,4},{6,7},{7,6},{8,9},{9,8},{10,11... | collective-permute-start | bytes 12582920 | tf_op jit(solution)/shard_map/ppermute | solution.py:174
  0.5 12.9 %collective-permute-start = (bf16[256,256]{1,0:T(8,128)(2,1)}, bf16[256,256]{1,0:T(8,128)(2,1)S(1)}, u32[]{:S(2)}, u32[]{:S(2)}) collective-permute-start(bf16[256,256]{1,0:T(8,128)(2,1)} %refs_0_.1), channel_id=1, source_target_pairs={{0,4},{1,5},{2,6},{3,7},{4,0},{5,1},{6,2},{7,3},{8,12},{9,13},{10,... | collective-permute-start | bytes 393224 | tf_op jit(solution)/shard_map/ppermute | solution.py:174
  4.0 11.5 %collective-permute-start.2 = (bf16[256,256]{1,0:T(8,128)(2,1)}, bf16[256,256]{1,0:T(8,128)(2,1)S(1)}, u32[]{:S(2)}, u32[]{:S(2)}) collective-permute-start(bf16[256,256]{1,0:T(8,128)(2,1)} %refs_0_.1), channel_id=1, source_target_pairs={{0,16},{1,9},{2,18},{3,11},{4,20},{5,13},{6,22},{7,15},{8,24},{9,1... | collective-permute-start | bytes 393224 | tf_op jit(solution)/shard_map/ppermute | solution.py:174
  5.6 10.0 %collective-permute-start.3 = (bf16[256,256]{1,0:T(8,128)(2,1)}, bf16[256,256]{1,0:T(8,128)(2,1)S(1)}, u32[]{:S(2)}, u32[]{:S(2)}) collective-permute-start(bf16[256,256]{1,0:T(8,128)(2,1)} %refs_0_.1), channel_id=1, source_target_pairs={{0,2},{1,3},{2,0},{3,1},{4,6},{5,7},{6,4},{7,5},{8,10},{9,11},{10,... | collective-permute-start | bytes 393224 | tf_op jit(solution)/shard_map/ppermute | solution.py:174
  7.1 7.7 %collective-permute-start.4 = (s32[2,4,16]{2,1,0:T(4,128)}, s32[2,4,16]{2,1,0:T(4,128)S(1)}, u32[]{:S(2)}, u32[]{:S(2)}) collective-permute-start(s32[2,4,16]{2,1,0:T(4,128)} %cols.1), channel_id=1, source_target_pairs={{0,1},{1,0},{2,3},{3,2},{4,5},{5,4},{6,7},{7,6},{8,9},{9,8},{10,11... | collective-permute-start | bytes 1544 | tf_op jit(solution)/shard_map/ppermute | solution.py:174
  14.5 11.1 %collective-permute-start.8 = (bf16[256,256]{1,0:T(8,128)(2,1)S(1)}, bf16[256,256]{1,0:T(8,128)(2,1)S(1)}, u32[]{:S(2)}, u32[]{:S(2)}) collective-permute-start(bf16[256,256]{1,0:T(8,128)(2,1)S(1)} %copy-done), channel_id=1, source_target_pairs={{0,8},{1,17},{2,10},{3,19},{4,12},{5,21},{6,14},{7,23},{8,0},{9,25... | collective-permute-start | bytes 393224 | tf_op jit(solution)/shard_map/ppermute | solution.py:174
  15.6 6.5 %collective-permute-start.9 = (bf16[256,256]{1,0:T(8,128)(2,1)S(1)}, bf16[256,256]{1,0:T(8,128)(2,1)S(1)}, u32[]{:S(2)}, u32[]{:S(2)}) collective-permute-start(bf16[256,256]{1,0:T(8,128)(2,1)S(1)} %collective-permute-done.2), channel_id=1, source_target_pairs={{0,2},{1,3},{2,0},{3,1},{4,6},{5,7},{6,4},{7,5},{8,10},{9,11},{10,... | collective-permute-start | bytes 393224 | tf_op jit(solution)/shard_map/ppermute | solution.py:174
  16.3 7.5 %collective-permute-start.10 = (bf16[256,256]{1,0:T(8,128)(2,1)S(1)}, bf16[256,256]{1,0:T(8,128)(2,1)S(1)}, u32[]{:S(2)}, u32[]{:S(2)}) collective-permute-start(bf16[256,256]{1,0:T(8,128)(2,1)S(1)} %collective-permute-done.refs_1_), channel_id=1, source_target_pairs={{0,2},{1,3},{2,0},{3,1},{4,6},{5,7},{6,4},{7,5},{8,10},{9,11},{10,... | collective-permute-start | bytes 393224 | tf_op jit(solution)/shard_map/ppermute | solution.py:174
  20.0 6.4 %collective-permute-start.7 = (bf16[512,256]{1,0:T(8,128)(2,1)S(1)}, bf16[512,256]{1,0:T(8,128)(2,1)S(1)}, u32[]{:S(2)}, u32[]{:S(2)}) collective-permute-start(bf16[512,256]{1,0:T(8,128)(2,1)S(1)} %constant_dynamic-update-slice_fusion.refs_2_), channel_id=1, source_target_pairs={{0,8},{1,17},{2,10},{3,19},{4,12},{5,21},{6,14},{7,23},{8,0},{9,25... | collective-permute-start | bytes 786440 | tf_op jit(solution)/shard_map/ppermute | solution.py:174
  21.4 7.7 %collective-permute-start.11 = (bf16[256,256]{1,0:T(8,128)(2,1)S(1)}, bf16[256,256]{1,0:T(8,128)(2,1)S(1)}, u32[]{:S(2)}, u32[]{:S(2)}) collective-permute-start(bf16[256,256]{1,0:T(8,128)(2,1)S(1)} %collective-permute-done.1.refs_5_), channel_id=1, source_target_pairs={{0,2},{1,3},{2,0},{3,1},{4,6},{5,7},{6,4},{7,5},{8,10},{9,11},{10,... | collective-permute-start | bytes 393224 | tf_op jit(solution)/shard_map/ppermute | solution.py:174
  22.1 8.6 %collective-permute-start.12 = (bf16[512,256]{1,0:T(8,128)(2,1)S(1)}, bf16[512,256]{1,0:T(8,128)(2,1)S(1)}, u32[]{:S(2)}, u32[]{:S(2)}) collective-permute-start(bf16[512,256]{1,0:T(8,128)(2,1)S(1)} %pad_maximum_fusion), channel_id=1, source_target_pairs={{0,8},{1,17},{2,10},{3,19},{4,12},{5,21},{6,14},{7,23},{8,0},{9,25... | collective-permute-start | bytes 786440 | tf_op jit(solution)/shard_map/ppermute | solution.py:174
  23.9 8.1 %collective-permute-start.13 = (bf16[512,256]{1,0:T(8,128)(2,1)S(1)}, bf16[512,256]{1,0:T(8,128)(2,1)S(1)}, u32[]{:S(2)}, u32[]{:S(2)}) collective-permute-start(bf16[512,256]{1,0:T(8,128)(2,1)S(1)} %pad_maximum_fusion.1), channel_id=1, source_target_pairs={{0,8},{1,17},{2,10},{3,19},{4,12},{5,21},{6,14},{7,23},{8,0},{9,25... | collective-permute-start | bytes 786440 | tf_op jit(solution)/shard_map/ppermute | solution.py:174
  36.1 9.4 %collective-permute-start.17 = (bf16[256,256]{1,0:T(8,128)(2,1)S(1)}, bf16[256,256]{1,0:T(8,128)(2,1)S(1)}, u32[]{:S(2)}, u32[]{:S(2)}) collective-permute-start(bf16[256,256]{1,0:T(8,128)(2,1)S(1)} %fusion.7.refs_0_), channel_id=1, source_target_pairs={{0,4},{1,5},{2,6},{3,7},{4,0},{5,1},{6,2},{7,3},{8,12},{9,13},{10,... | collective-permute-start | bytes 393224 | tf_op jit(solution)/shard_map/ppermute | solution.py:174
  36.7 10.0 %collective-permute-start.16 = (bf16[256,256]{1,0:T(8,128)(2,1)S(1)}, bf16[256,256]{1,0:T(8,128)(2,1)S(1)}, u32[]{:S(2)}, u32[]{:S(2)}) collective-permute-start(bf16[256,256]{1,0:T(8,128)(2,1)S(1)} %fusion.7.refs_0_), channel_id=1, source_target_pairs={{0,16},{1,9},{2,18},{3,11},{4,20},{5,13},{6,22},{7,15},{8,24},{9,1... | collective-permute-start | bytes 393224 | tf_op jit(solution)/shard_map/ppermute | solution.py:174
  37.7 9.0 %collective-permute-start.18 = (bf16[256,256]{1,0:T(8,128)(2,1)S(1)}, bf16[256,256]{1,0:T(8,128)(2,1)S(1)}, u32[]{:S(2)}, u32[]{:S(2)}) collective-permute-start(bf16[256,256]{1,0:T(8,128)(2,1)S(1)} %fusion.7.refs_0_), channel_id=1, source_target_pairs={{0,2},{1,3},{2,0},{3,1},{4,6},{5,7},{6,4},{7,5},{8,10},{9,11},{10,... | collective-permute-start | bytes 393224 | tf_op jit(solution)/shard_map/ppermute | solution.py:174
  45.5 5.8 %collective-permute-start.21 = (bf16[256,256]{1,0:T(8,128)(2,1)S(1)}, bf16[256,256]{1,0:T(8,128)(2,1)S(1)}, u32[]{:S(2)}, u32[]{:S(2)}) collective-permute-start(bf16[256,256]{1,0:T(8,128)(2,1)S(1)} %collective-permute-done.17.refs_0_), channel_id=1, source_target_pairs={{0,16},{1,9},{2,18},{3,11},{4,20},{5,13},{6,22},{7,15},{8,24},{9,1... | collective-permute-start | bytes 393224 | tf_op jit(solution)/shard_map/ppermute | solution.py:174
  47.1 6.5 %collective-permute-start.19 = (bf16[256,256]{1,0:T(8,128)(2,1)S(1)}, bf16[256,256]{1,0:T(8,128)(2,1)S(1)}, u32[]{:S(2)}, u32[]{:S(2)}) collective-permute-start(bf16[256,256]{1,0:T(8,128)(2,1)S(1)} %collective-permute-done.16), channel_id=1, source_target_pairs={{0,2},{1,3},{2,0},{3,1},{4,6},{5,7},{6,4},{7,5},{8,10},{9,11},{10,... | collective-permute-start | bytes 393224 | tf_op jit(solution)/shard_map/ppermute | solution.py:174
  47.2 9.2 %collective-permute-start.20 = (bf16[256,256]{1,0:T(8,128)(2,1)S(1)}, bf16[256,256]{1,0:T(8,128)(2,1)S(1)}, u32[]{:S(2)}, u32[]{:S(2)}) collective-permute-start(bf16[256,256]{1,0:T(8,128)(2,1)S(1)} %collective-permute-done.17.refs_0_), channel_id=1, source_target_pairs={{0,2},{1,3},{2,0},{3,1},{4,6},{5,7},{6,4},{7,5},{8,10},{9,11},{10,... | collective-permute-start | bytes 393224 | tf_op jit(solution)/shard_map/ppermute | solution.py:174
  49.2 7.5 %collective-permute-start.24 = (bf16[256,256]{1,0:T(8,128)(2,1)S(1)}, bf16[256,256]{1,0:T(8,128)(2,1)S(1)}, u32[]{:S(2)}, u32[]{:S(2)}) collective-permute-start(bf16[256,256]{1,0:T(8,128)(2,1)S(1)} %fusion.7.refs_0_), channel_id=1, source_target_pairs={{0,8},{1,17},{2,10},{3,19},{4,12},{5,21},{6,14},{7,23},{8,0},{9,25... | collective-permute-start | bytes 393224 | tf_op jit(solution)/shard_map/ppermute | solution.py:174
  49.5 7.5 %collective-permute-start.23 = (bf16[512,256]{1,0:T(8,128)(2,1)S(1)}, bf16[512,256]{1,0:T(8,128)(2,1)S(1)}, u32[]{:S(2)}, u32[]{:S(2)}) collective-permute-start(bf16[512,256]{1,0:T(8,128)(2,1)S(1)} %constant_dynamic-update-slice_fusion.2.refs_1_), channel_id=1, source_target_pairs={{0,8},{1,17},{2,10},{3,19},{4,12},{5,21},{6,14},{7,23},{8,0},{9,25... | collective-permute-start | bytes 786440 | tf_op jit(solution)/shard_map/ppermute | solution.py:174
  51.3 6.6 %collective-permute-start.22 = (bf16[256,256]{1,0:T(8,128)(2,1)S(1)}, bf16[256,256]{1,0:T(8,128)(2,1)S(1)}, u32[]{:S(2)}, u32[]{:S(2)}) collective-permute-start(bf16[256,256]{1,0:T(8,128)(2,1)S(1)} %collective-permute-done.21.refs_2_), channel_id=1, source_target_pairs={{0,2},{1,3},{2,0},{3,1},{4,6},{5,7},{6,4},{7,5},{8,10},{9,11},{10,... | collective-permute-start | bytes 393224 | tf_op jit(solution)/shard_map/ppermute | solution.py:174
  53.6 6.4 %collective-permute-start.25 = (bf16[512,256]{1,0:T(8,128)(2,1)S(1)}, bf16[512,256]{1,0:T(8,128)(2,1)S(1)}, u32[]{:S(2)}, u32[]{:S(2)}) collective-permute-start(bf16[512,256]{1,0:T(8,128)(2,1)S(1)} %pad_maximum_fusion.2), channel_id=1, source_target_pairs={{0,8},{1,17},{2,10},{3,19},{4,12},{5,21},{6,14},{7,23},{8,0},{9,25... | collective-permute-start | bytes 786440 | tf_op jit(solution)/shard_map/ppermute | solution.py:174
  56.4 6.4 %collective-permute-start.26 = (bf16[512,256]{1,0:T(8,128)(2,1)S(1)}, bf16[512,256]{1,0:T(8,128)(2,1)S(1)}, u32[]{:S(2)}, u32[]{:S(2)}) collective-permute-start(bf16[512,256]{1,0:T(8,128)(2,1)S(1)} %pad_maximum_fusion.3), channel_id=1, source_target_pairs={{0,8},{1,17},{2,10},{3,19},{4,12},{5,21},{6,14},{7,23},{8,0},{9,25... | collective-permute-start | bytes 786440 | tf_op jit(solution)/shard_map/ppermute | solution.py:174
  57.9 6.4 %collective-permute-start.27 = (bf16[256,256]{1,0:T(8,128)(2,1)S(1)}, bf16[256,256]{1,0:T(8,128)(2,1)S(1)}, u32[]{:S(2)}, u32[]{:S(2)}) collective-permute-start(bf16[256,256]{1,0:T(8,128)(2,1)S(1)} %collective-permute-done.22.refs_2_), channel_id=1, source_target_pairs={{0,8},{1,17},{2,10},{3,19},{4,12},{5,21},{6,14},{7,23},{8,0},{9,25... | collective-permute-start | bytes 393224 | tf_op jit(solution)/shard_map/ppermute | solution.py:174
  (11 other events, 23.1 us)

commit v3 on v2

--- a/solution.py
+++ b/solution.py
@@ -9,6 +9,20 @@
 from jax.sharding import PartitionSpec as P
 
 HOPS = 2
+PLANS = (
+    {'after': {'f1': [], 'f2': ['A0'], 'f3': ['A1'], 'r': ['A0'], 's0': [], 't0': ['A1'], 't3': ['A2']},
+     'anchors': {'A0': [], 'A1': ['q', 'f0'], 'A2': ['f2', 't0', 's0', 'f0']},
+     'corner': False,
+     'expand1': 'A0',
+     'expand2': 'A1',
+     'last': ['t3'],
+     'steps': ['q', 'f0', 'p', 'A0', 'f2', 'r', 'f1', 'A1', 't0', 's0', 'f3', 't1', 't2', 'A2', 't3']},
+    {'after': {'t3': ['A2']},
+     'anchors': {'A2': ['f2', 'r']},
+     'corner': False,
+     'last': ['t1', 't2', 't3'],
+     'steps': ['s0', 'q', 'p', 'r', 'f0', 'f1', 'f2', 't0', 'f3', 't1', 'A2', 't2', 't3']},
+)
 VLIM = 48 << 20
 AXES = ("blk", "rep")
 LONG = pl.CostEstimate(flops=0, bytes_accessed=1 << 32, transcendentals=0)
@@ -30,10 +44,10 @@
 
 def expand_kernel(lanes_of, cols, counts, core, tiles, *refs, members, counting):
     if counting:
-        wanted, dense, restart, token, sem = refs
+        wanted, _, dense, restart, sem = refs
+    else:
+        dense, token, sem = refs
         token[...] = jnp.zeros_like(token)
-    else:
-        _, dense, sem = refs
     blocks_dev, panels, _, bs, _ = tiles.shape
     dense[...] = jnp.zeros_like(dense)
     mine = core[0]
@@ -75,23 +89,25 @@
     blocks_dev, panels, slots, bs, _ = tiles.shape
     rows = blocks_dev * bs
     columns = lanes_of.shape[0] // 2 * rows
+    counting = wanted is not None
     smem, vmem = pl.BlockSpec(memory_space=pltpu.SMEM), pl.BlockSpec(memory_space=pltpu.VMEM)
-    counting = wanted is not None
     out_shape = [jax.ShapeDtypeStruct((rows, columns), tiles.dtype)]
     if counting:
         out_shape.append(jax.ShapeDtypeStruct((rows, wanted.shape[1]), jnp.float32))
+    else:
         out_shape.append(jax.ShapeDtypeStruct((8, 128), jnp.float32))
     return pl.pallas_call(
         functools.partial(expand_kernel, members=members, counting=counting),
         out_shape=out_shape,
         in_specs=[smem] * 4
-        + [pl.BlockSpec(memory_space=pltpu.HBM), vmem if counting else pl.BlockSpec(memory_space=pl.ANY)],
-        out_specs=[vmem] * len(out_shape),
+        + [pl.BlockSpec(memory_space=pltpu.HBM)]
+        + [vmem, pl.BlockSpec(memory_space=pl.ANY)] * counting,
+        out_specs=[vmem] * 2,
         scratch_shapes=[pltpu.SemaphoreType.DMA],
         compiler_params=pltpu.CompilerParams(vmem_limit_bytes=VLIM),
         cost_estimate=LONG,
         name="expand_blocks",
-    )(lanes_of, cols, counts, core, tiles, wanted if counting else token)
+    )(lanes_of, cols, counts, core, tiles, *([wanted, token] if counting else []))
 
 
 def pause(value):
@@ -156,7 +172,10 @@
     second = {
         j: pairs(lambda y, x, z, c: (y + j, x, z, c) if c else (y, x + j, z, c)) for j in range(1, side)
     }
-    return along, first, second, pairs(lambda y, x, z, c: (y, x, z, 1 - c))
+    corner = {
+        j: pairs(lambda y, x, z, c: (y, x + j, z ^ 1, c) if c else (y + j, x, z ^ 1, c)) for j in range(1, side)
+    }
+    return along, first, second, corner, pairs(lambda y, x, z, c: (y, x, z, 1 - c))
 
 
 def per_device(scores, tiles, cols, counts, seeds):
@@ -168,7 +187,7 @@
     member = lax.axis_index("rep")
     lanes_of = piece_lanes(panel, member, side, members, rows_dev).astype(jnp.int32)
     core = jnp.stack([member % 2, (panel * members + member) * rows_dev]).astype(jnp.int32)
-    along, first, second, across = permutes(side, depth)
+    along, first, second, corner, across = permutes(side, depth)
 
     def send(value, pairs):
         return lax.ppermute(value, AXES, pairs)
@@ -191,48 +210,88 @@
 
     current = scores
     for hop_index in range(HOPS):
-        o = current
-        q = send(o, along[2])
-        f0 = joined([send(o, first[a]) for a in steps])
-        p = send(o, along[1])
-        s0 = [send(o, second[b]) for b in steps]
-        if hop_index:
-            total = multiply(both, [(lane(0), o)])
-            q = after(q, total)
-        else:
-            half, restart, token = expand(lanes_of, cols, counts, core, tiles, members, seeds.T)
-            q = after(q, half)
-        f2 = joined([send(q, first[a]) for a in steps])
-        m0 = joined([f0, p])
-        early = [(lane(runs[1] + side - 1), q), (lane(runs[0]), m0)]
-        if hop_index:
-            anchor = total = multiply(both, early, total)
-        else:
-            anchor = token = pause(after(token, q, f0, p, *others))
-        f2 = after(f2, anchor)
-        r = send(after(q, anchor), along[1])
-        f1 = send(after(f0, anchor), along[1])
-        t0 = [send(after(m0, anchor), second[b]) for b in steps]
-        f3 = send(f2, along[1])
-        m1, m2 = joined([after(f1, f2), q]), joined([f2, r])
-        t1 = [send(m1, second[b]) for b in steps]
-        t2 = [send(m2, second[b]) for b in steps]
-        later = stepped(runs[0], side, t0) + [(lane(b), s) for b, s in zip(steps, s0)] + [(lane(runs[2]), f2)]
-        if hop_index:
-            anchor = total = multiply(both, later, total)
-        else:
-            given = after(lanes_of, f2, *t0, *s0)
-            both = [*expand(given, others[0], others[1], core, others[2], members, token=token), half]
-            anchor = both[0]
-            later = [(lane(0), o), *early, *later]
-        f3 = after(f3, anchor)
-        t3 = [send(f3, second[b]) for b in steps]
-        items = [(lane(runs[1]), f1), (lane(runs[2] + side - 1), r), (lane(runs[3]), f3)]
-        items += stepped(runs[1], side, t1) + stepped(runs[2], side, t2)
-        total = multiply(both, items, total) if hop_index else multiply(both, later + items)
+        plan = PLANS[hop_index]
+        v = {"o": current}
+
+        def tied(name, stage):
+            value = v[name]
+            ties = [anchor for n, anchor in anchors if n in plan["after"].get(stage, ())]
+            return after(value, *ties) if ties else value
+
+        anchors = []
+
+        def do(stage):
+            if stage in v:
+                return
+            if stage == "q":
+                v["q"] = send(tied("o", "q"), along[2])
+            elif stage == "f0":
+                v["f0"] = joined([send(tied("o", "f0"), first[a]) for a in steps])
+            elif stage == "p":
+                v["p"] = send(tied("o", "p"), along[1])
+            elif stage == "s0":
+                v["s0"] = joined([send(tied("o", "s0"), second[b]) for b in steps])
+            elif stage == "f1":
+                v["f1"] = send(tied("f0", "f1"), along[1])
+            elif stage == "t0":
+                v["m0"] = joined([v["f0"], v["p"]])
+                v["t0"] = joined([send(tied("m0", "t0"), second[b]) for b in steps])
+            elif stage == "f2":
+                v["f2"] = joined([send(tied("q", "f2"), first[a]) for a in steps])
+            elif stage == "r":
+                v["r"] = send(tied("q", "r"), along[1])
+            elif stage == "f3":
+                if plan["corner"]:
+                    v["f3"] = joined([send(tied("q", "f3"), corner[a]) for a in steps])
+                else:
+                    v["f3"] = send(tied("f2", "f3"), along[1])
+            elif stage == "t1":
+                v["m1"] = joined([v["f1"], v["q"]])
+                v["t1"] = joined([send(tied("m1", "t1"), second[b]) for b in steps])
+            elif stage == "t2":
+                v["m2"] = joined([v["f2"], v["r"]])
+                v["t2"] = joined([send(tied("m2", "t2"), second[b]) for b in steps])
+            elif stage == "t3":
+                v["t3"] = joined([send(tied("f3", "t3"), second[b]) for b in steps])
+
+        places = {
+            "o": lane(0), "s0": lane(1), "m0": lane(runs[0]), "t0": lane(runs[0] + side), "q": lane(runs[1] + side - 1),
+            "f1": lane(runs[1]), "t1": lane(runs[1] + side), "f2": lane(runs[2]), "r": lane(runs[2] + side - 1),
+            "t2": lane(runs[2] + side), "f3": lane(runs[3]), "t3": lane(runs[3] + side - 1),
+        }
+        left = ["o", "s0", "m0", "t0", "q", "f1", "t1", "f2", "r", "t2", "f3", "t3"]
+        total = None
+        for step in plan["steps"]:
+            if step[0] != "A":
+                do(step)
+                continue
+            names = plan["anchors"][step]
+            if hop_index:
+                take = [n for n in names if n in left]
+                for n in take:
+                    left.remove(n)
+                total = multiply(both, [(places[n], v[n]) for n in take], total)
+                anchors.append((step, total))
+            elif step == plan["expand1"]:
+                held = pause(others[2])
+                tables = after(others[0], held), after(others[1], held)
+                half, token = expand(lanes_of, *tables, core, held, members)
+                anchors.append((step, half))
+            elif step == plan["expand2"]:
+                given = after(lanes_of, *[v[n] for n in names])
+                own, restart = expand(given, cols, counts, core, tiles, members, seeds.T, token)
+                both = [half, own]
+                anchors.append((step, own))
+            else:
+                token = pause(after(token, *[v[n] for n in names]))
+                anchors.append((step, token))
+        last = plan["last"]
+        items = [(places[n], v[n]) for n in left if n not in last]
+        total = multiply(both, items, total)
         theirs, mine = total[:rows_dev], total[rows_dev:]
-        for start, value in stepped(runs[3], side - 1, t3):
-            at = slice(start, start + value.shape[0])
+        for n in last:
+            value = v[n]
+            at = slice(places[n], places[n] + value.shape[0])
             theirs += jnp.dot(both[0][:, at], value, preferred_element_type=jnp.float32)
             mine += jnp.dot(both[1][:, at], value, preferred_element_type=jnp.float32)
         summed = mine + send(theirs, across)

time: 67.3 us -> 64.9 us (0.964)
  local copies, waits for them, and re-layouts: 3.39 us -> 0.06 us
  matrix products: 0.73 us -> 1.66 us
  Pallas kernels: 8.29 us -> 7.59 us
    unnamed x14 -> x10, local copies, waits for them, and re-layouts: 3.37 us -> 0.04 us
    pallas_call x5 -> x3, Pallas kernels: 2.88 us -> 2.27 us  [multiply(): pl.pallas_call(functools.partial(multiply_kernel, places=places, added=bo...]
  transfers between devices with their start and end apart: 29 -> 29, of which waited for: 17 -> 14; matrix products, arithmetic and copies ran while one was open for 1% -> 2% of each run, Pallas kernels for 12% -> 12%
where the time goes in v3:
time: 64.9 us; the launch traced here: 64 us
  starting transfers between devices  27.4 us (42%)
  waiting for transfers between devices  26 us (40%)
  Pallas kernels  7.59 us (12%)
  matrix products  1.66 us (3%)
  other arithmetic  1 us (2%)
    ppermute x29, starting transfers between devices, send(): return lax.ppermute(value, AXES, pairs)  27.4 us
    ppermute x29, waiting for transfers between devices, send(): return lax.ppermute(value, AXES, pairs)  26 us
    pallas_call x2, Pallas kernels, expand(): pl.pallas_call(functools.partial(expand_kernel, members=members, counting...  5.32 us
    pallas_call x3, Pallas kernels, multiply(): pl.pallas_call(functools.partial(multiply_kernel, places=places, added=bo...  2.27 us
  transfers between devices with their start and end apart: 29, of which 14 were waited for; matrix products, arithmetic and copies ran while one was open for 2% of the time, Pallas kernels for 12%

profile of v3, /device:TPU:0, one launch (start us, length us, event | category | flops | bytes accessed | tf_op | source)
XLA Modules:
  0.0 64.0 jit_solution(13160877598333240640)
XLA Ops:
  0.5 3.6 %collective-permute-start.3 = (bf16[256,256]{1,0:T(8,128)(2,1)}, bf16[256,256]{1,0:T(8,128)(2,1)S(1)}, u32[]{:S(2)}, u32[]{:S(2)}) collective-permute-start(bf16[256,256]{1,0:T(8,128)(2,1)} %refs_0_.1), channel_id=1, source_target_pairs={{0,4},{1,5},{2,6},{3,7},{4,0},{5,1},{6,2},{7,3},{8,12},{9,13},{10,... | collective-permute-start | bytes 393224 | tf_op jit(solution)/shard_map/ppermute | solution.py:193
  4.0 1.5 %collective-permute-start.4 = (bf16[256,256]{1,0:T(8,128)(2,1)}, bf16[256,256]{1,0:T(8,128)(2,1)S(1)}, u32[]{:S(2)}, u32[]{:S(2)}) collective-permute-start(bf16[256,256]{1,0:T(8,128)(2,1)} %refs_0_.1), channel_id=1, source_target_pairs={{0,16},{1,9},{2,18},{3,11},{4,20},{5,13},{6,22},{7,15},{8,24},{9,1... | collective-permute-start | bytes 393224 | tf_op jit(solution)/shard_map/ppermute | solution.py:193
  5.6 1.6 %collective-permute-start.6 = (bf16[256,256]{1,0:T(8,128)(2,1)}, bf16[256,256]{1,0:T(8,128)(2,1)S(1)}, u32[]{:S(2)}, u32[]{:S(2)}) collective-permute-start(bf16[256,256]{1,0:T(8,128)(2,1)} %refs_0_.1), channel_id=1, source_target_pairs={{0,2},{1,3},{2,0},{3,1},{4,6},{5,7},{6,4},{7,5},{8,10},{9,11},{10,... | collective-permute-start | bytes 393224 | tf_op jit(solution)/shard_map/ppermute | solution.py:193
  7.2 2.0 %collective-permute-done.4 = bf16[256,256]{1,0:T(8,128)(2,1)S(1)} collective-permute-done((bf16[256,256]{1,0:T(8,128)(2,1)}, bf16[256,256]{1,0:T(8,128)(2,1)S(1)}, u32[]{:S(2)}, u32[]{:S(2)}) %collective-permute-start.4) | collective-permute-done | bytes 131104 | tf_op jit(solution)/shard_map/ppermute | solution.py:193
  9.2 1.6 %collective-permute-start.8 = (bf16[256,256]{1,0:T(8,128)(2,1)S(1)}, bf16[256,256]{1,0:T(8,128)(2,1)S(1)}, u32[]{:S(2)}, u32[]{:S(2)}) collective-permute-start(bf16[256,256]{1,0:T(8,128)(2,1)S(1)} %collective-permute-done.4), channel_id=1, source_target_pairs={{0,2},{1,3},{2,0},{3,1},{4,6},{5,7},{6,4},{7,5},{8,10},{9,11},{10,... | collective-permute-start | bytes 393224 | tf_op jit(solution)/shard_map/ppermute | solution.py:193
  11.0 1.3 %collective-permute-done.2.counts = s32[2,4]{1,0:T(2,128)S(1)} collective-permute-done((s32[2,4]{1,0:T(2,128)}, s32[2,4]{1,0:T(2,128)S(1)}, u32[]{:S(2)}, u32[]{:S(2)}) %collective-permute-start.2) | collective-permute-done | bytes 64 | tf_op jit(solution)/shard_map/ppermute | solution.py:193
  12.2 1.9 %expand_blocks.2 = (bf16[256,4096]{1,0:T(8,128)(2,1)S(1)}, f32[8,128]{1,0:T(8,128)S(1)}) custom-call(s32[32]{0:T(128)S(1)} %fusion.39.lanes_of, s32[2,4,16]{2,1,0:T(4,128)S(1)} %collective-permute-done.cols, s32[2,4]{1,0:T(2,128)S(1)} %collective-permute-done.2.counts, s32[2]{0:T(128)S(1)} %pad_add_fusion.core, bf16[2,4,16,128,128]{4,3,2,1,0:T(8,128)(2,1)} %pause.2.tiles), custom_call_target="tpu_custom_call" | custom-call | bytes 4294967296 | tf_op jit(solution)/shard_map/expand_blocks/pallas_call | solution.py:99
  14.2 1.9 %collective-permute-start.10 = (bf16[256,256]{1,0:T(8,128)(2,1)S(1)}, bf16[256,256]{1,0:T(8,128)(2,1)S(1)}, u32[]{:S(2)}, u32[]{:S(2)}) collective-permute-start(bf16[256,256]{1,0:T(8,128)(2,1)S(1)} %collective-permute-done.3.refs_4_), channel_id=1, source_target_pairs={{0,16},{1,9},{2,18},{3,11},{4,20},{5,13},{6,22},{7,15},{8,24},{9,1... | collective-permute-start | bytes 393224 | tf_op jit(solution)/shard_map/ppermute | solution.py:193
  16.4 1.4 %collective-permute-start.9 = (bf16[512,256]{1,0:T(8,128)(2,1)S(1)}, bf16[512,256]{1,0:T(8,128)(2,1)S(1)}, u32[]{:S(2)}, u32[]{:S(2)}) collective-permute-start(bf16[512,256]{1,0:T(8,128)(2,1)S(1)} %pad_maximum_fusion), channel_id=1, source_target_pairs={{0,8},{1,17},{2,10},{3,19},{4,12},{5,21},{6,14},{7,23},{8,0},{9,25... | collective-permute-start | bytes 786440 | tf_op jit(solution)/shard_map/ppermute | solution.py:193
  17.8 3.4 %expand_blocks.3 = (bf16[256,4096]{1,0:T(8,128)(2,1)S(1)}, f32[256,256]{1,0:T(8,128)S(1)}) custom-call(s32[32]{0:T(128)S(1)} %fusion.39.lanes_of, s32[2,4,16]{2,1,0:T(4,128)S(1)} %copy-done.2, s32[2,4]{1,0:T(2,128)S(1)} %copy-done.3, s32[2]{0:T(128)S(1)} %pad_add_fusion.core, bf16[2,4,16,128,128]{4,3,2,1,0:T(8,128)(2,1)} %tiles.1, s32[16,256]{1,0:T(8,128)S(1)} %bitcast.11, ...), custom_call_target="tpu_custom_call" | custom-call | bytes 4294967296 | tf_op jit(solution)/shard_map/expand_blocks/pallas_call | solution.py:99
  22.4 2.0 %collective-permute-start.12 = (bf16[512,256]{1,0:T(8,128)(2,1)S(1)}, bf16[512,256]{1,0:T(8,128)(2,1)S(1)}, u32[]{:S(2)}, u32[]{:S(2)}) collective-permute-start(bf16[512,256]{1,0:T(8,128)(2,1)S(1)} %pad_maximum_fusion.1), channel_id=1, source_target_pairs={{0,8},{1,17},{2,10},{3,19},{4,12},{5,21},{6,14},{7,23},{8,0},{9,25... | collective-permute-start | bytes 786440 | tf_op jit(solution)/shard_map/ppermute | solution.py:193
  24.5 1.8 %collective-permute-done.13.refs_10_ = bf16[256,256]{1,0:T(8,128)(2,1)S(1)} collective-permute-done((bf16[256,256]{1,0:T(8,128)(2,1)S(1)}, bf16[256,256]{1,0:T(8,128)(2,1)S(1)}, u32[]{:S(2)}, u32[]{:S(2)}) %collective-permute-start.13) | collective-permute-done | bytes 131104 | tf_op jit(solution)/shard_map/ppermute | solution.py:193
  26.4 1.9 %collective-permute-start.14 = (bf16[256,256]{1,0:T(8,128)(2,1)S(1)}, bf16[256,256]{1,0:T(8,128)(2,1)S(1)}, u32[]{:S(2)}, u32[]{:S(2)}) collective-permute-start(bf16[256,256]{1,0:T(8,128)(2,1)S(1)} %collective-permute-done.13.refs_10_), channel_id=1, source_target_pairs={{0,8},{1,17},{2,10},{3,19},{4,12},{5,21},{6,14},{7,23},{8,0},{9,25... | collective-permute-start | bytes 393224 | tf_op jit(solution)/shard_map/ppermute | solution.py:193
  28.3 3.6 %collective-permute-done.5.refs_1_ = bf16[256,256]{1,0:T(8,128)(2,1)S(1)} collective-permute-done((bf16[256,256]{1,0:T(8,128)(2,1)S(1)}, bf16[256,256]{1,0:T(8,128)(2,1)S(1)}, u32[]{:S(2)}, u32[]{:S(2)}) %collective-permute-start.5) | collective-permute-done | bytes 131104 | tf_op jit(solution)/shard_map/ppermute | solution.py:193
  31.9 1.2 %multiply_pieces.3 = f32[512,256]{1,0:T(8,128)S(1)} custom-call(bf16[256,4096]{1,0:T(8,128)(2,1)S(1)} %get-tuple-element.18.theirs, bf16[256,4096]{1,0:T(8,128)(2,1)S(1)} %get-tuple-element.21.mine, bf16[256,256]{1,0:T(8,128)(2,1)S(1)} %copy-done, bf16[256,256]{1,0:T(8,128)(2,1)S(1)} %collective-permute-done.5.refs_1_, ...), custom_call_target="tpu_custom_call" | custom-call | bytes 4294967296 | tf_op jit(solution)/shard_map/multiply_pieces/pallas_call | solution.py:145
  33.7 1.3 %collective-permute-done.15 = f32[256,256]{1,0:T(8,128)S(1)} collective-permute-done((f32[256,256]{1,0:T(8,128)S(1)}, f32[256,256]{1,0:T(8,128)S(1)}, u32[]{:S(2)}, u32[]{:S(2)}) %collective-permute-start.15) | collective-permute-done | bytes 262176 | tf_op jit(solution)/shard_map/ppermute | solution.py:193
  37.2 3.0 %collective-permute-done.17 = bf16[256,256]{1,0:T(8,128)(2,1)S(1)} collective-permute-done((bf16[256,256]{1,0:T(8,128)(2,1)S(1)}, bf16[256,256]{1,0:T(8,128)(2,1)S(1)}, u32[]{:S(2)}, u32[]{:S(2)}) %collective-permute-start.17) | collective-permute-done | bytes 131104 | tf_op jit(solution)/shard_map/ppermute | solution.py:193
  41.2 2.4 %collective-permute-done.18 = bf16[256,256]{1,0:T(8,128)(2,1)S(1)} collective-permute-done((bf16[256,256]{1,0:T(8,128)(2,1)S(1)}, bf16[256,256]{1,0:T(8,128)(2,1)S(1)}, u32[]{:S(2)}, u32[]{:S(2)}) %collective-permute-start.18) | collective-permute-done | bytes 131104 | tf_op jit(solution)/shard_map/ppermute | solution.py:193
  45.5 1.4 %collective-permute-start.24 = (bf16[256,256]{1,0:T(8,128)(2,1)S(1)}, bf16[256,256]{1,0:T(8,128)(2,1)S(1)}, u32[]{:S(2)}, u32[]{:S(2)}) collective-permute-start(bf16[256,256]{1,0:T(8,128)(2,1)S(1)} %collective-permute-done.20.refs_4_), channel_id=1, source_target_pairs={{0,2},{1,3},{2,0},{3,1},{4,6},{5,7},{6,4},{7,5},{8,10},{9,11},{10,... | collective-permute-start | bytes 393224 | tf_op jit(solution)/shard_map/ppermute | solution.py:193
  46.8 1.3 %collective-permute-start.25 = (bf16[512,256]{1,0:T(8,128)(2,1)S(1)}, bf16[512,256]{1,0:T(8,128)(2,1)S(1)}, u32[]{:S(2)}, u32[]{:S(2)}) collective-permute-start(bf16[512,256]{1,0:T(8,128)(2,1)S(1)} %pad_maximum_fusion.2), channel_id=1, source_target_pairs={{0,8},{1,17},{2,10},{3,19},{4,12},{5,21},{6,14},{7,23},{8,0},{9,25... | collective-permute-start | bytes 786440 | tf_op jit(solution)/shard_map/ppermute | solution.py:193
  48.9 2.6 %collective-permute-done.22.refs_0_ = bf16[256,256]{1,0:T(8,128)(2,1)S(1)} collective-permute-done((bf16[256,256]{1,0:T(8,128)(2,1)S(1)}, bf16[256,256]{1,0:T(8,128)(2,1)S(1)}, u32[]{:S(2)}, u32[]{:S(2)}) %collective-permute-start.22) | collective-permute-done | bytes 131104 | tf_op jit(solution)/shard_map/ppermute | solution.py:193
  53.2 3.3 %collective-permute-done.23.refs_6_ = bf16[256,256]{1,0:T(8,128)(2,1)S(1)} collective-permute-done((bf16[256,256]{1,0:T(8,128)(2,1)S(1)}, bf16[256,256]{1,0:T(8,128)(2,1)S(1)}, u32[]{:S(2)}, u32[]{:S(2)}) %collective-permute-start.23) | collective-permute-done | bytes 131104 | tf_op jit(solution)/shard_map/ppermute | solution.py:193
  56.5 1.4 %collective-permute-start.27 = (bf16[256,256]{1,0:T(8,128)(2,1)S(1)}, bf16[256,256]{1,0:T(8,128)(2,1)S(1)}, u32[]{:S(2)}, u32[]{:S(2)}) collective-permute-start(bf16[256,256]{1,0:T(8,128)(2,1)S(1)} %collective-permute-done.23.refs_6_), channel_id=1, source_target_pairs={{0,8},{1,17},{2,10},{3,19},{4,12},{5,21},{6,14},{7,23},{8,0},{9,25... | collective-permute-start | bytes 393224 | tf_op jit(solution)/shard_map/ppermute | solution.py:193
  59.1 2.3 %collective-permute-done.27 = bf16[256,256]{1,0:T(8,128)(2,1)S(1)} collective-permute-done((bf16[256,256]{1,0:T(8,128)(2,1)S(1)}, bf16[256,256]{1,0:T(8,128)(2,1)S(1)}, u32[]{:S(2)}, u32[]{:S(2)}) %collective-permute-start.27) | collective-permute-done | bytes 131104 | tf_op jit(solution)/shard_map/ppermute | solution.py:193
  (68 shorter events, 14.1 us)
Async XLA Ops:
  0.0 10.8 %collective-permute-start.1 = (bf16[2,4,16,128,128]{4,3,2,1,0:T(8,128)(2,1)}, bf16[2,4,16,128,128]{4,3,2,1,0:T(8,128)(2,1)}, u32[]{:S(2)}, u32[]{:S(2)}) collective-permute-start(bf16[2,4,16,128,128]{4,3,2,1,0:T(8,128)(2,1)} %tiles.1), channel_id=1, source_target_pairs={{0,1},{1,0},{2,3},{3,2},{4,5},{5,4},{6,7},{7,6},{8,9},{9,8},{10,11... | collective-permute-start | bytes 12582920 | tf_op jit(solution)/shard_map/ppermute | solution.py:193
  0.5 13.7 %collective-permute-start.3 = (bf16[256,256]{1,0:T(8,128)(2,1)}, bf16[256,256]{1,0:T(8,128)(2,1)S(1)}, u32[]{:S(2)}, u32[]{:S(2)}) collective-permute-start(bf16[256,256]{1,0:T(8,128)(2,1)} %refs_0_.1), channel_id=1, source_target_pairs={{0,4},{1,5},{2,6},{3,7},{4,0},{5,1},{6,2},{7,3},{8,12},{9,13},{10,... | collective-permute-start | bytes 393224 | tf_op jit(solution)/shard_map/ppermute | solution.py:193
  4.0 5.2 %collective-permute-start.4 = (bf16[256,256]{1,0:T(8,128)(2,1)}, bf16[256,256]{1,0:T(8,128)(2,1)S(1)}, u32[]{:S(2)}, u32[]{:S(2)}) collective-permute-start(bf16[256,256]{1,0:T(8,128)(2,1)} %refs_0_.1), channel_id=1, source_target_pairs={{0,16},{1,9},{2,18},{3,11},{4,20},{5,13},{6,22},{7,15},{8,24},{9,1... | collective-permute-start | bytes 393224 | tf_op jit(solution)/shard_map/ppermute | solution.py:193
  5.6 10.8 %collective-permute-start.6 = (bf16[256,256]{1,0:T(8,128)(2,1)}, bf16[256,256]{1,0:T(8,128)(2,1)S(1)}, u32[]{:S(2)}, u32[]{:S(2)}) collective-permute-start(bf16[256,256]{1,0:T(8,128)(2,1)} %refs_0_.1), channel_id=1, source_target_pairs={{0,2},{1,3},{2,0},{3,1},{4,6},{5,7},{6,4},{7,5},{8,10},{9,11},{10,... | collective-permute-start | bytes 393224 | tf_op jit(solution)/shard_map/ppermute | solution.py:193
  9.2 7.2 %collective-permute-start.8 = (bf16[256,256]{1,0:T(8,128)(2,1)S(1)}, bf16[256,256]{1,0:T(8,128)(2,1)S(1)}, u32[]{:S(2)}, u32[]{:S(2)}) collective-permute-start(bf16[256,256]{1,0:T(8,128)(2,1)S(1)} %collective-permute-done.4), channel_id=1, source_target_pairs={{0,2},{1,3},{2,0},{3,1},{4,6},{5,7},{6,4},{7,5},{8,10},{9,11},{10,... | collective-permute-start | bytes 393224 | tf_op jit(solution)/shard_map/ppermute | solution.py:193
  14.2 7.1 %collective-permute-start.10 = (bf16[256,256]{1,0:T(8,128)(2,1)S(1)}, bf16[256,256]{1,0:T(8,128)(2,1)S(1)}, u32[]{:S(2)}, u32[]{:S(2)}) collective-permute-start(bf16[256,256]{1,0:T(8,128)(2,1)S(1)} %collective-permute-done.3.refs_4_), channel_id=1, source_target_pairs={{0,16},{1,9},{2,18},{3,11},{4,20},{5,13},{6,22},{7,15},{8,24},{9,1... | collective-permute-start | bytes 393224 | tf_op jit(solution)/shard_map/ppermute | solution.py:193
  16.1 6.3 %collective-permute-start.11 = (bf16[256,256]{1,0:T(8,128)(2,1)S(1)}, bf16[256,256]{1,0:T(8,128)(2,1)S(1)}, u32[]{:S(2)}, u32[]{:S(2)}) collective-permute-start(bf16[256,256]{1,0:T(8,128)(2,1)S(1)} %collective-permute-done.3.refs_4_), channel_id=1, source_target_pairs={{0,2},{1,3},{2,0},{3,1},{4,6},{5,7},{6,4},{7,5},{8,10},{9,11},{10,... | collective-permute-start | bytes 393224 | tf_op jit(solution)/shard_map/ppermute | solution.py:193
  16.4 15.5 %collective-permute-start.9 = (bf16[512,256]{1,0:T(8,128)(2,1)S(1)}, bf16[512,256]{1,0:T(8,128)(2,1)S(1)}, u32[]{:S(2)}, u32[]{:S(2)}) collective-permute-start(bf16[512,256]{1,0:T(8,128)(2,1)S(1)} %pad_maximum_fusion), channel_id=1, source_target_pairs={{0,8},{1,17},{2,10},{3,19},{4,12},{5,21},{6,14},{7,23},{8,0},{9,25... | collective-permute-start | bytes 786440 | tf_op jit(solution)/shard_map/ppermute | solution.py:193
  21.2 10.7 %collective-permute-start.7 = (bf16[512,256]{1,0:T(8,128)(2,1)S(1)}, bf16[512,256]{1,0:T(8,128)(2,1)S(1)}, u32[]{:S(2)}, u32[]{:S(2)}) collective-permute-start(bf16[512,256]{1,0:T(8,128)(2,1)S(1)} %constant_dynamic-update-slice_fusion.refs_2_), channel_id=1, source_target_pairs={{0,8},{1,17},{2,10},{3,19},{4,12},{5,21},{6,14},{7,23},{8,0},{9,25... | collective-permute-start | bytes 786440 | tf_op jit(solution)/shard_map/ppermute | solution.py:193
  21.3 5.0 %collective-permute-start.13 = (bf16[256,256]{1,0:T(8,128)(2,1)S(1)}, bf16[256,256]{1,0:T(8,128)(2,1)S(1)}, u32[]{:S(2)}, u32[]{:S(2)}) collective-permute-start(bf16[256,256]{1,0:T(8,128)(2,1)S(1)} %collective-permute-done.10.refs_7_), channel_id=1, source_target_pairs={{0,2},{1,3},{2,0},{3,1},{4,6},{5,7},{6,4},{7,5},{8,10},{9,11},{10,... | collective-permute-start | bytes 393224 | tf_op jit(solution)/shard_map/ppermute | solution.py:193
  22.4 9.5 %collective-permute-start.12 = (bf16[512,256]{1,0:T(8,128)(2,1)S(1)}, bf16[512,256]{1,0:T(8,128)(2,1)S(1)}, u32[]{:S(2)}, u32[]{:S(2)}) collective-permute-start(bf16[512,256]{1,0:T(8,128)(2,1)S(1)} %pad_maximum_fusion.1), channel_id=1, source_target_pairs={{0,8},{1,17},{2,10},{3,19},{4,12},{5,21},{6,14},{7,23},{8,0},{9,25... | collective-permute-start | bytes 786440 | tf_op jit(solution)/shard_map/ppermute | solution.py:193
  24.4 7.5 %collective-permute-start.5 = (bf16[256,256]{1,0:T(8,128)(2,1)S(1)}, bf16[256,256]{1,0:T(8,128)(2,1)S(1)}, u32[]{:S(2)}, u32[]{:S(2)}) collective-permute-start(bf16[256,256]{1,0:T(8,128)(2,1)S(1)} %copy-done), channel_id=1, source_target_pairs={{0,8},{1,17},{2,10},{3,19},{4,12},{5,21},{6,14},{7,23},{8,0},{9,25... | collective-permute-start | bytes 393224 | tf_op jit(solution)/shard_map/ppermute | solution.py:193
  26.4 6.9 %collective-permute-start.14 = (bf16[256,256]{1,0:T(8,128)(2,1)S(1)}, bf16[256,256]{1,0:T(8,128)(2,1)S(1)}, u32[]{:S(2)}, u32[]{:S(2)}) collective-permute-start(bf16[256,256]{1,0:T(8,128)(2,1)S(1)} %collective-permute-done.13.refs_10_), channel_id=1, source_target_pairs={{0,8},{1,17},{2,10},{3,19},{4,12},{5,21},{6,14},{7,23},{8,0},{9,25... | collective-permute-start | bytes 393224 | tf_op jit(solution)/shard_map/ppermute | solution.py:193
  35.2 5.0 %collective-permute-start.17 = (bf16[256,256]{1,0:T(8,128)(2,1)S(1)}, bf16[256,256]{1,0:T(8,128)(2,1)S(1)}, u32[]{:S(2)}, u32[]{:S(2)}) collective-permute-start(bf16[256,256]{1,0:T(8,128)(2,1)S(1)} %fusion.11.refs_0_), channel_id=1, source_target_pairs={{0,16},{1,9},{2,18},{3,11},{4,20},{5,13},{6,22},{7,15},{8,24},{9,1... | collective-permute-start | bytes 393224 | tf_op jit(solution)/shard_map/ppermute | solution.py:193
  35.2 8.4 %collective-permute-start.18 = (bf16[256,256]{1,0:T(8,128)(2,1)S(1)}, bf16[256,256]{1,0:T(8,128)(2,1)S(1)}, u32[]{:S(2)}, u32[]{:S(2)}) collective-permute-start(bf16[256,256]{1,0:T(8,128)(2,1)S(1)} %fusion.11.refs_0_), channel_id=1, source_target_pairs={{0,2},{1,3},{2,0},{3,1},{4,6},{5,7},{6,4},{7,5},{8,10},{9,11},{10,... | collective-permute-start | bytes 393224 | tf_op jit(solution)/shard_map/ppermute | solution.py:193
  36.3 9.1 %collective-permute-start.20 = (bf16[256,256]{1,0:T(8,128)(2,1)S(1)}, bf16[256,256]{1,0:T(8,128)(2,1)S(1)}, u32[]{:S(2)}, u32[]{:S(2)}) collective-permute-start(bf16[256,256]{1,0:T(8,128)(2,1)S(1)} %fusion.11.refs_0_), channel_id=1, source_target_pairs={{0,4},{1,5},{2,6},{3,7},{4,0},{5,1},{6,2},{7,3},{8,12},{9,13},{10,... | collective-permute-start | bytes 393224 | tf_op jit(solution)/shard_map/ppermute | solution.py:193
  40.2 6.6 %collective-permute-start.21 = (bf16[256,256]{1,0:T(8,128)(2,1)S(1)}, bf16[256,256]{1,0:T(8,128)(2,1)S(1)}, u32[]{:S(2)}, u32[]{:S(2)}) collective-permute-start(bf16[256,256]{1,0:T(8,128)(2,1)S(1)} %collective-permute-done.17), channel_id=1, source_target_pairs={{0,2},{1,3},{2,0},{3,1},{4,6},{5,7},{6,4},{7,5},{8,10},{9,11},{10,... | collective-permute-start | bytes 393224 | tf_op jit(solution)/shard_map/ppermute | solution.py:193
  43.6 14.2 %collective-permute-start.19 = (bf16[512,256]{1,0:T(8,128)(2,1)S(1)}, bf16[512,256]{1,0:T(8,128)(2,1)S(1)}, u32[]{:S(2)}, u32[]{:S(2)}) collective-permute-start(bf16[512,256]{1,0:T(8,128)(2,1)S(1)} %constant_dynamic-update-slice_fusion.2.refs_2_), channel_id=1, source_target_pairs={{0,8},{1,17},{2,10},{3,19},{4,12},{5,21},{6,14},{7,23},{8,0},{9,25... | collective-permute-start | bytes 786440 | tf_op jit(solution)/shard_map/ppermute | solution.py:193
  45.4 6.1 %collective-permute-start.22 = (bf16[256,256]{1,0:T(8,128)(2,1)S(1)}, bf16[256,256]{1,0:T(8,128)(2,1)S(1)}, u32[]{:S(2)}, u32[]{:S(2)}) collective-permute-start(bf16[256,256]{1,0:T(8,128)(2,1)S(1)} %collective-permute-done.20.refs_4_), channel_id=1, source_target_pairs={{0,16},{1,9},{2,18},{3,11},{4,20},{5,13},{6,22},{7,15},{8,24},{9,1... | collective-permute-start | bytes 393224 | tf_op jit(solution)/shard_map/ppermute | solution.py:193
  45.5 6.2 %collective-permute-start.24 = (bf16[256,256]{1,0:T(8,128)(2,1)S(1)}, bf16[256,256]{1,0:T(8,128)(2,1)S(1)}, u32[]{:S(2)}, u32[]{:S(2)}) collective-permute-start(bf16[256,256]{1,0:T(8,128)(2,1)S(1)} %collective-permute-done.20.refs_4_), channel_id=1, source_target_pairs={{0,2},{1,3},{2,0},{3,1},{4,6},{5,7},{6,4},{7,5},{8,10},{9,11},{10,... | collective-permute-start | bytes 393224 | tf_op jit(solution)/shard_map/ppermute | solution.py:193
  46.8 11.8 %collective-permute-start.25 = (bf16[512,256]{1,0:T(8,128)(2,1)S(1)}, bf16[512,256]{1,0:T(8,128)(2,1)S(1)}, u32[]{:S(2)}, u32[]{:S(2)}) collective-permute-start(bf16[512,256]{1,0:T(8,128)(2,1)S(1)} %pad_maximum_fusion.2), channel_id=1, source_target_pairs={{0,8},{1,17},{2,10},{3,19},{4,12},{5,21},{6,14},{7,23},{8,0},{9,25... | collective-permute-start | bytes 786440 | tf_op jit(solution)/shard_map/ppermute | solution.py:193
  48.2 9.7 %collective-permute-start.16 = (bf16[256,256]{1,0:T(8,128)(2,1)S(1)}, bf16[256,256]{1,0:T(8,128)(2,1)S(1)}, u32[]{:S(2)}, u32[]{:S(2)}) collective-permute-start(bf16[256,256]{1,0:T(8,128)(2,1)S(1)} %fusion.11.refs_0_), channel_id=1, source_target_pairs={{0,8},{1,17},{2,10},{3,19},{4,12},{5,21},{6,14},{7,23},{8,0},{9,25... | collective-permute-start | bytes 393224 | tf_op jit(solution)/shard_map/ppermute | solution.py:193
  51.5 5.0 %collective-permute-start.23 = (bf16[256,256]{1,0:T(8,128)(2,1)S(1)}, bf16[256,256]{1,0:T(8,128)(2,1)S(1)}, u32[]{:S(2)}, u32[]{:S(2)}) collective-permute-start(bf16[256,256]{1,0:T(8,128)(2,1)S(1)} %collective-permute-done.22.refs_0_), channel_id=1, source_target_pairs={{0,2},{1,3},{2,0},{3,1},{4,6},{5,7},{6,4},{7,5},{8,10},{9,11},{10,... | collective-permute-start | bytes 393224 | tf_op jit(solution)/shard_map/ppermute | solution.py:193
  51.7 7.2 %collective-permute-start.26 = (bf16[512,256]{1,0:T(8,128)(2,1)S(1)}, bf16[512,256]{1,0:T(8,128)(2,1)S(1)}, u32[]{:S(2)}, u32[]{:S(2)}) collective-permute-start(bf16[512,256]{1,0:T(8,128)(2,1)S(1)} %pad_maximum_fusion.3), channel_id=1, source_target_pairs={{0,8},{1,17},{2,10},{3,19},{4,12},{5,21},{6,14},{7,23},{8,0},{9,25... | collective-permute-start | bytes 786440 | tf_op jit(solution)/shard_map/ppermute | solution.py:193
  (9 other events, 40.7 us)

commit v4 on v3

--- a/solution.py
+++ b/solution.py
@@ -10,18 +10,18 @@
 
 HOPS = 2
 PLANS = (
-    {'after': {'f1': [], 'f2': ['A0'], 'f3': ['A1'], 'r': ['A0'], 's0': [], 't0': ['A1'], 't3': ['A2']},
-     'anchors': {'A0': [], 'A1': ['q', 'f0'], 'A2': ['f2', 't0', 's0', 'f0']},
+    {'after': {'f1': [], 'f2': ['A0'], 'f3': ['A1'], 'r': ['A0'], 's0': [], 't0': [], 't3': ['A2']},
+     'anchors': {'A0': [], 'A1': ['q', 'f0', 'f1'], 'A2': ['f2', 't0'], 'A54': ['f0']},
      'corner': False,
      'expand1': 'A0',
      'expand2': 'A1',
      'last': ['t3'],
-     'steps': ['q', 'f0', 'p', 'A0', 'f2', 'r', 'f1', 'A1', 't0', 's0', 'f3', 't1', 't2', 'A2', 't3']},
-    {'after': {'t3': ['A2']},
-     'anchors': {'A2': ['f2', 'r']},
+     'steps': ['q', 'p', 'A0', 'f0', 'r', 'f1', 'A1', 'f2', 's0', 't1', 'f3', 'A54', 't0', 't2', 'A2', 't3']},
+    {'after': {'f3': ['A76'], 't3': ['A2', 'A76']},
+     'anchors': {'A2': ['f2', 'r'], 'A76': ['q', 'f1']},
      'corner': False,
      'last': ['t1', 't2', 't3'],
-     'steps': ['s0', 'q', 'p', 'r', 'f0', 'f1', 'f2', 't0', 'f3', 't1', 'A2', 't2', 't3']},
+     'steps': ['p', 'q', 's0', 'r', 'f0', 'f1', 'f2', 'A76', 't0', 'A2', 'f3', 't1', 't3', 't2']},
 )
 VLIM = 48 << 20
 AXES = ("blk", "rep")

time: 64.9 us -> 63.1 us (0.972); the launches traced: 64 us -> 63 us
  Pallas kernels: 7.59 us -> 9.44 us
  waiting for transfers between devices: 26 us -> 24.2 us
  starting transfers between devices: 27.4 us -> 26.3 us
    ppermute x29, waiting for transfers between devices: 26 us -> 24.2 us  [send(): return lax.ppermute(value, AXES, pairs)]
    pallas_call x2, Pallas kernels: 5.32 us -> 6.99 us  [expand(): pl.pallas_call(functools.partial(expand_kernel, members=members, counting...]
    ppermute x29, starting transfers between devices: 27.4 us -> 26.3 us  [send(): return lax.ppermute(value, AXES, pairs)]
    pallas_call x3 -> x4, Pallas kernels: 2.27 us -> 2.45 us  [multiply(): pl.pallas_call(functools.partial(multiply_kernel, places=places, added=bo...]
  transfers between devices with their start and end apart: 29 -> 29, of which waited for: 14 -> 15; matrix products, arithmetic and copies ran while one was open for 2% -> 2% of each run, Pallas kernels for 12% -> 15%
where the time goes in v4:
time: 63.1 us; the launch traced here: 63 us
  starting transfers between devices  26.3 us (42%)
  waiting for transfers between devices  24.2 us (38%)
  Pallas kernels  9.44 us (15%)
  matrix products  1.65 us (3%)
  other arithmetic  1 us (2%)
    ppermute x29, starting transfers between devices, send(): return lax.ppermute(value, AXES, pairs)  26.3 us
    ppermute x29, waiting for transfers between devices, send(): return lax.ppermute(value, AXES, pairs)  24.2 us
    pallas_call x2, Pallas kernels, expand(): pl.pallas_call(functools.partial(expand_kernel, members=members, counting...  6.99 us
    pallas_call x4, Pallas kernels, multiply(): pl.pallas_call(functools.partial(multiply_kernel, places=places, added=bo...  2.45 us
  transfers between devices with their start and end apart: 29, of which 15 were waited for; matrix products, arithmetic and copies ran while one was open for 2% of the time, Pallas kernels for 15%

profile of v4, /device:TPU:0, one launch (start us, length us, event | category | flops | bytes accessed | tf_op | source)
XLA Modules:
  0.0 63.0 jit_solution(685076429077243246)
XLA Ops:
  0.5 2.5 %collective-permute-start.4 = (bf16[256,256]{1,0:T(8,128)(2,1)}, bf16[256,256]{1,0:T(8,128)(2,1)S(1)}, u32[]{:S(2)}, u32[]{:S(2)}) collective-permute-start(bf16[256,256]{1,0:T(8,128)(2,1)} %refs_0_.1), channel_id=1, source_target_pairs={{0,16},{1,9},{2,18},{3,11},{4,20},{5,13},{6,22},{7,15},{8,24},{9,1... | collective-permute-start | bytes 393224 | tf_op jit(solution)/shard_map/ppermute | solution.py:193
  3.0 2.6 %collective-permute-start.3 = (bf16[256,256]{1,0:T(8,128)(2,1)}, bf16[256,256]{1,0:T(8,128)(2,1)S(1)}, u32[]{:S(2)}, u32[]{:S(2)}) collective-permute-start(bf16[256,256]{1,0:T(8,128)(2,1)} %refs_0_.1), channel_id=1, source_target_pairs={{0,4},{1,5},{2,6},{3,7},{4,0},{5,1},{6,2},{7,3},{8,12},{9,13},{10,... | collective-permute-start | bytes 393224 | tf_op jit(solution)/shard_map/ppermute | solution.py:193
  5.6 1.6 %collective-permute-start.7 = (bf16[256,256]{1,0:T(8,128)(2,1)}, bf16[256,256]{1,0:T(8,128)(2,1)S(1)}, u32[]{:S(2)}, u32[]{:S(2)}) collective-permute-start(bf16[256,256]{1,0:T(8,128)(2,1)} %refs_0_.1), channel_id=1, source_target_pairs={{0,2},{1,3},{2,0},{3,1},{4,6},{5,7},{6,4},{7,5},{8,10},{9,11},{10,... | collective-permute-start | bytes 393224 | tf_op jit(solution)/shard_map/ppermute | solution.py:193
  9.6 2.7 %expand_blocks.2 = (bf16[256,4096]{1,0:T(8,128)(2,1)S(1)}, f32[8,128]{1,0:T(8,128)S(1)}) custom-call(s32[32]{0:T(128)S(1)} %fusion.39.lanes_of, s32[2,4,16]{2,1,0:T(4,128)S(1)} %collective-permute-done.cols, s32[2,4]{1,0:T(2,128)S(1)} %collective-permute-done.2.counts, s32[2]{0:T(128)S(1)} %pad_add_fusion.core, bf16[2,4,16,128,128]{4,3,2,1,0:T(8,128)(2,1)} %pause.3.tiles), custom_call_target="tpu_custom_call" | custom-call | bytes 4294967296 | tf_op jit(solution)/shard_map/expand_blocks/pallas_call | solution.py:99
  12.6 1.3 %collective-permute-start.10 = (bf16[256,256]{1,0:T(8,128)(2,1)S(1)}, bf16[256,256]{1,0:T(8,128)(2,1)S(1)}, u32[]{:S(2)}, u32[]{:S(2)}) collective-permute-start(bf16[256,256]{1,0:T(8,128)(2,1)S(1)} %collective-permute-done.3.refs_4_), channel_id=1, source_target_pairs={{0,16},{1,9},{2,18},{3,11},{4,20},{5,13},{6,22},{7,15},{8,24},{9,1... | collective-permute-start | bytes 393224 | tf_op jit(solution)/shard_map/ppermute | solution.py:193
  13.9 1.5 %collective-permute-start.11 = (bf16[256,256]{1,0:T(8,128)(2,1)S(1)}, bf16[256,256]{1,0:T(8,128)(2,1)S(1)}, u32[]{:S(2)}, u32[]{:S(2)}) collective-permute-start(bf16[256,256]{1,0:T(8,128)(2,1)S(1)} %collective-permute-done.3.refs_4_), channel_id=1, source_target_pairs={{0,2},{1,3},{2,0},{3,1},{4,6},{5,7},{6,4},{7,5},{8,10},{9,11},{10,... | collective-permute-start | bytes 393224 | tf_op jit(solution)/shard_map/ppermute | solution.py:193
  15.4 1.4 %collective-permute-start.8 = (bf16[512,256]{1,0:T(8,128)(2,1)S(1)}, bf16[512,256]{1,0:T(8,128)(2,1)S(1)}, u32[]{:S(2)}, u32[]{:S(2)}) collective-permute-start(bf16[512,256]{1,0:T(8,128)(2,1)S(1)} %constant_dynamic-update-slice_fusion.refs_2_), channel_id=1, source_target_pairs={{0,8},{1,17},{2,10},{3,19},{4,12},{5,21},{6,14},{7,23},{8,0},{9,25... | collective-permute-start | bytes 786440 | tf_op jit(solution)/shard_map/ppermute | solution.py:193
  17.6 4.3 %expand_blocks.3 = (bf16[256,4096]{1,0:T(8,128)(2,1)S(1)}, f32[256,256]{1,0:T(8,128)S(1)}) custom-call(s32[32]{0:T(128)S(1)} %fusion.39.lanes_of, s32[2,4,16]{2,1,0:T(4,128)S(1)} %copy-done.2, s32[2,4]{1,0:T(2,128)S(1)} %copy-done.3, s32[2]{0:T(128)S(1)} %pad_add_fusion.core, bf16[2,4,16,128,128]{4,3,2,1,0:T(8,128)(2,1)} %tiles.1, s32[16,256]{1,0:T(8,128)S(1)} %bitcast.11, ...), custom_call_target="tpu_custom_call" | custom-call | bytes 4294967296 | tf_op jit(solution)/shard_map/expand_blocks/pallas_call | solution.py:99
  22.5 1.6 %collective-permute-start.6 = (bf16[256,256]{1,0:T(8,128)(2,1)S(1)}, bf16[256,256]{1,0:T(8,128)(2,1)S(1)}, u32[]{:S(2)}, u32[]{:S(2)}) collective-permute-start(bf16[256,256]{1,0:T(8,128)(2,1)S(1)} %copy-done), channel_id=1, source_target_pairs={{0,8},{1,17},{2,10},{3,19},{4,12},{5,21},{6,14},{7,23},{8,0},{9,25... | collective-permute-start | bytes 393224 | tf_op jit(solution)/shard_map/ppermute | solution.py:193
  24.1 2.8 %collective-permute-done.13.refs_10_ = bf16[256,256]{1,0:T(8,128)(2,1)S(1)} collective-permute-done((bf16[256,256]{1,0:T(8,128)(2,1)S(1)}, bf16[256,256]{1,0:T(8,128)(2,1)S(1)}, u32[]{:S(2)}, u32[]{:S(2)}) %collective-permute-start.13) | collective-permute-done | bytes 131104 | tf_op jit(solution)/shard_map/ppermute | solution.py:193
  26.9 2.9 %collective-permute-done.6.refs_1_ = bf16[256,256]{1,0:T(8,128)(2,1)S(1)} collective-permute-done((bf16[256,256]{1,0:T(8,128)(2,1)S(1)}, bf16[256,256]{1,0:T(8,128)(2,1)S(1)}, u32[]{:S(2)}, u32[]{:S(2)}) %collective-permute-start.6) | collective-permute-done | bytes 131104 | tf_op jit(solution)/shard_map/ppermute | solution.py:193
  32.3 1.3 %collective-permute-done.15 = f32[256,256]{1,0:T(8,128)S(1)} collective-permute-done((f32[256,256]{1,0:T(8,128)S(1)}, f32[256,256]{1,0:T(8,128)S(1)}, u32[]{:S(2)}, u32[]{:S(2)}) %collective-permute-start.15) | collective-permute-done | bytes 262176 | tf_op jit(solution)/shard_map/ppermute | solution.py:193
  33.8 1.4 %collective-permute-start.18 = (bf16[256,256]{1,0:T(8,128)(2,1)S(1)}, bf16[256,256]{1,0:T(8,128)(2,1)S(1)}, u32[]{:S(2)}, u32[]{:S(2)}) collective-permute-start(bf16[256,256]{1,0:T(8,128)(2,1)S(1)} %fusion.11.refs_0_), channel_id=1, source_target_pairs={{0,2},{1,3},{2,0},{3,1},{4,6},{5,7},{6,4},{7,5},{8,10},{9,11},{10,... | collective-permute-start | bytes 393224 | tf_op jit(solution)/shard_map/ppermute | solution.py:193
  35.3 1.2 %collective-permute-start.20 = (bf16[256,256]{1,0:T(8,128)(2,1)S(1)}, bf16[256,256]{1,0:T(8,128)(2,1)S(1)}, u32[]{:S(2)}, u32[]{:S(2)}) collective-permute-start(bf16[256,256]{1,0:T(8,128)(2,1)S(1)} %fusion.11.refs_0_), channel_id=1, source_target_pairs={{0,4},{1,5},{2,6},{3,7},{4,0},{5,1},{6,2},{7,3},{8,12},{9,13},{10,... | collective-permute-start | bytes 393224 | tf_op jit(solution)/shard_map/ppermute | solution.py:193
  36.5 2.3 %collective-permute-done.17 = bf16[256,256]{1,0:T(8,128)(2,1)S(1)} collective-permute-done((bf16[256,256]{1,0:T(8,128)(2,1)S(1)}, bf16[256,256]{1,0:T(8,128)(2,1)S(1)}, u32[]{:S(2)}, u32[]{:S(2)}) %collective-permute-start.17) | collective-permute-done | bytes 131104 | tf_op jit(solution)/shard_map/ppermute | solution.py:193
  38.8 1.4 %collective-permute-start.22 = (bf16[256,256]{1,0:T(8,128)(2,1)S(1)}, bf16[256,256]{1,0:T(8,128)(2,1)S(1)}, u32[]{:S(2)}, u32[]{:S(2)}) collective-permute-start(bf16[256,256]{1,0:T(8,128)(2,1)S(1)} %collective-permute-done.17), channel_id=1, source_target_pairs={{0,2},{1,3},{2,0},{3,1},{4,6},{5,7},{6,4},{7,5},{8,10},{9,11},{10,... | collective-permute-start | bytes 393224 | tf_op jit(solution)/shard_map/ppermute | solution.py:193
  40.2 2.2 %collective-permute-done.18 = bf16[256,256]{1,0:T(8,128)(2,1)S(1)} collective-permute-done((bf16[256,256]{1,0:T(8,128)(2,1)S(1)}, bf16[256,256]{1,0:T(8,128)(2,1)S(1)}, u32[]{:S(2)}, u32[]{:S(2)}) %collective-permute-start.18) | collective-permute-done | bytes 131104 | tf_op jit(solution)/shard_map/ppermute | solution.py:193
  42.5 1.6 %collective-permute-done.20.refs_0_ = bf16[256,256]{1,0:T(8,128)(2,1)S(1)} collective-permute-done((bf16[256,256]{1,0:T(8,128)(2,1)S(1)}, bf16[256,256]{1,0:T(8,128)(2,1)S(1)}, u32[]{:S(2)}, u32[]{:S(2)}) %collective-permute-start.20) | collective-permute-done | bytes 131104 | tf_op jit(solution)/shard_map/ppermute | solution.py:193
  44.3 2.1 %collective-permute-start.24 = (bf16[256,256]{1,0:T(8,128)(2,1)S(1)}, bf16[256,256]{1,0:T(8,128)(2,1)S(1)}, u32[]{:S(2)}, u32[]{:S(2)}) collective-permute-start(bf16[256,256]{1,0:T(8,128)(2,1)S(1)} %collective-permute-done.20.refs_0_), channel_id=1, source_target_pairs={{0,2},{1,3},{2,0},{3,1},{4,6},{5,7},{6,4},{7,5},{8,10},{9,11},{10,... | collective-permute-start | bytes 393224 | tf_op jit(solution)/shard_map/ppermute | solution.py:193
  47.4 1.2 %collective-permute-start.16 = (bf16[256,256]{1,0:T(8,128)(2,1)S(1)}, bf16[256,256]{1,0:T(8,128)(2,1)S(1)}, u32[]{:S(2)}, u32[]{:S(2)}) collective-permute-start(bf16[256,256]{1,0:T(8,128)(2,1)S(1)} %fusion.11.refs_0_), channel_id=1, source_target_pairs={{0,8},{1,17},{2,10},{3,19},{4,12},{5,21},{6,14},{7,23},{8,0},{9,25... | collective-permute-start | bytes 393224 | tf_op jit(solution)/shard_map/ppermute | solution.py:193
  48.9 1.6 %collective-permute-done.21.refs_0_ = bf16[256,256]{1,0:T(8,128)(2,1)S(1)} collective-permute-done((bf16[256,256]{1,0:T(8,128)(2,1)S(1)}, bf16[256,256]{1,0:T(8,128)(2,1)S(1)}, u32[]{:S(2)}, u32[]{:S(2)}) %collective-permute-start.21) | collective-permute-done | bytes 131104 | tf_op jit(solution)/shard_map/ppermute | solution.py:193
  50.8 1.6 %collective-permute-start.26 = (bf16[512,256]{1,0:T(8,128)(2,1)S(1)}, bf16[512,256]{1,0:T(8,128)(2,1)S(1)}, u32[]{:S(2)}, u32[]{:S(2)}) collective-permute-start(bf16[512,256]{1,0:T(8,128)(2,1)S(1)} %pad_maximum_fusion.3), channel_id=1, source_target_pairs={{0,8},{1,17},{2,10},{3,19},{4,12},{5,21},{6,14},{7,23},{8,0},{9,25... | collective-permute-start | bytes 786440 | tf_op jit(solution)/shard_map/ppermute | solution.py:193
  52.7 2.7 %collective-permute-done.23.refs_4_ = bf16[256,256]{1,0:T(8,128)(2,1)S(1)} collective-permute-done((bf16[256,256]{1,0:T(8,128)(2,1)S(1)}, bf16[256,256]{1,0:T(8,128)(2,1)S(1)}, u32[]{:S(2)}, u32[]{:S(2)}) %collective-permute-start.23) | collective-permute-done | bytes 131104 | tf_op jit(solution)/shard_map/ppermute | solution.py:193
  57.5 3.0 %collective-permute-done.27 = bf16[256,256]{1,0:T(8,128)(2,1)S(1)} collective-permute-done((bf16[256,256]{1,0:T(8,128)(2,1)S(1)}, bf16[256,256]{1,0:T(8,128)(2,1)S(1)}, u32[]{:S(2)}, u32[]{:S(2)}) %collective-permute-start.27) | collective-permute-done | bytes 131104 | tf_op jit(solution)/shard_map/ppermute | solution.py:193
  (70 shorter events, 13.7 us)
Async XLA Ops:
  0.0 8.2 %collective-permute-start.1 = (bf16[2,4,16,128,128]{4,3,2,1,0:T(8,128)(2,1)}, bf16[2,4,16,128,128]{4,3,2,1,0:T(8,128)(2,1)}, u32[]{:S(2)}, u32[]{:S(2)}) collective-permute-start(bf16[2,4,16,128,128]{4,3,2,1,0:T(8,128)(2,1)} %tiles.1), channel_id=1, source_target_pairs={{0,1},{1,0},{2,3},{3,2},{4,5},{5,4},{6,7},{7,6},{8,9},{9,8},{10,11... | collective-permute-start | bytes 12582920 | tf_op jit(solution)/shard_map/ppermute | solution.py:193
  0.5 6.8 %collective-permute-start.4 = (bf16[256,256]{1,0:T(8,128)(2,1)}, bf16[256,256]{1,0:T(8,128)(2,1)S(1)}, u32[]{:S(2)}, u32[]{:S(2)}) collective-permute-start(bf16[256,256]{1,0:T(8,128)(2,1)} %refs_0_.1), channel_id=1, source_target_pairs={{0,16},{1,9},{2,18},{3,11},{4,20},{5,13},{6,22},{7,15},{8,24},{9,1... | collective-permute-start | bytes 393224 | tf_op jit(solution)/shard_map/ppermute | solution.py:193
  3.0 9.6 %collective-permute-start.3 = (bf16[256,256]{1,0:T(8,128)(2,1)}, bf16[256,256]{1,0:T(8,128)(2,1)S(1)}, u32[]{:S(2)}, u32[]{:S(2)}) collective-permute-start(bf16[256,256]{1,0:T(8,128)(2,1)} %refs_0_.1), channel_id=1, source_target_pairs={{0,4},{1,5},{2,6},{3,7},{4,0},{5,1},{6,2},{7,3},{8,12},{9,13},{10,... | collective-permute-start | bytes 393224 | tf_op jit(solution)/shard_map/ppermute | solution.py:193
  5.6 9.8 %collective-permute-start.7 = (bf16[256,256]{1,0:T(8,128)(2,1)}, bf16[256,256]{1,0:T(8,128)(2,1)S(1)}, u32[]{:S(2)}, u32[]{:S(2)}) collective-permute-start(bf16[256,256]{1,0:T(8,128)(2,1)} %refs_0_.1), channel_id=1, source_target_pairs={{0,2},{1,3},{2,0},{3,1},{4,6},{5,7},{6,4},{7,5},{8,10},{9,11},{10,... | collective-permute-start | bytes 393224 | tf_op jit(solution)/shard_map/ppermute | solution.py:193
  7.3 9.6 %collective-permute-start.5 = (bf16[256,256]{1,0:T(8,128)(2,1)S(1)}, bf16[256,256]{1,0:T(8,128)(2,1)S(1)}, u32[]{:S(2)}, u32[]{:S(2)}) collective-permute-start(bf16[256,256]{1,0:T(8,128)(2,1)S(1)} %collective-permute-done.4), channel_id=1, source_target_pairs={{0,2},{1,3},{2,0},{3,1},{4,6},{5,7},{6,4},{7,5},{8,10},{9,11},{10,... | collective-permute-start | bytes 393224 | tf_op jit(solution)/shard_map/ppermute | solution.py:193
  12.6 9.3 %collective-permute-start.10 = (bf16[256,256]{1,0:T(8,128)(2,1)S(1)}, bf16[256,256]{1,0:T(8,128)(2,1)S(1)}, u32[]{:S(2)}, u32[]{:S(2)}) collective-permute-start(bf16[256,256]{1,0:T(8,128)(2,1)S(1)} %collective-permute-done.3.refs_4_), channel_id=1, source_target_pairs={{0,16},{1,9},{2,18},{3,11},{4,20},{5,13},{6,22},{7,15},{8,24},{9,1... | collective-permute-start | bytes 393224 | tf_op jit(solution)/shard_map/ppermute | solution.py:193
  13.9 8.1 %collective-permute-start.11 = (bf16[256,256]{1,0:T(8,128)(2,1)S(1)}, bf16[256,256]{1,0:T(8,128)(2,1)S(1)}, u32[]{:S(2)}, u32[]{:S(2)}) collective-permute-start(bf16[256,256]{1,0:T(8,128)(2,1)S(1)} %collective-permute-done.3.refs_4_), channel_id=1, source_target_pairs={{0,2},{1,3},{2,0},{3,1},{4,6},{5,7},{6,4},{7,5},{8,10},{9,11},{10,... | collective-permute-start | bytes 393224 | tf_op jit(solution)/shard_map/ppermute | solution.py:193
  15.4 14.4 %collective-permute-start.8 = (bf16[512,256]{1,0:T(8,128)(2,1)S(1)}, bf16[512,256]{1,0:T(8,128)(2,1)S(1)}, u32[]{:S(2)}, u32[]{:S(2)}) collective-permute-start(bf16[512,256]{1,0:T(8,128)(2,1)S(1)} %constant_dynamic-update-slice_fusion.refs_2_), channel_id=1, source_target_pairs={{0,8},{1,17},{2,10},{3,19},{4,12},{5,21},{6,14},{7,23},{8,0},{9,25... | collective-permute-start | bytes 786440 | tf_op jit(solution)/shard_map/ppermute | solution.py:193
  16.9 13.0 %collective-permute-start.9 = (bf16[512,256]{1,0:T(8,128)(2,1)S(1)}, bf16[512,256]{1,0:T(8,128)(2,1)S(1)}, u32[]{:S(2)}, u32[]{:S(2)}) collective-permute-start(bf16[512,256]{1,0:T(8,128)(2,1)S(1)} %pad_maximum_fusion), channel_id=1, source_target_pairs={{0,8},{1,17},{2,10},{3,19},{4,12},{5,21},{6,14},{7,23},{8,0},{9,25... | collective-permute-start | bytes 786440 | tf_op jit(solution)/shard_map/ppermute | solution.py:193
  21.9 5.0 %collective-permute-start.13 = (bf16[256,256]{1,0:T(8,128)(2,1)S(1)}, bf16[256,256]{1,0:T(8,128)(2,1)S(1)}, u32[]{:S(2)}, u32[]{:S(2)}) collective-permute-start(bf16[256,256]{1,0:T(8,128)(2,1)S(1)} %collective-permute-done.10.refs_7_), channel_id=1, source_target_pairs={{0,2},{1,3},{2,0},{3,1},{4,6},{5,7},{6,4},{7,5},{8,10},{9,11},{10,... | collective-permute-start | bytes 393224 | tf_op jit(solution)/shard_map/ppermute | solution.py:193
  22.0 7.9 %collective-permute-start.12 = (bf16[512,256]{1,0:T(8,128)(2,1)S(1)}, bf16[512,256]{1,0:T(8,128)(2,1)S(1)}, u32[]{:S(2)}, u32[]{:S(2)}) collective-permute-start(bf16[512,256]{1,0:T(8,128)(2,1)S(1)} %pad_maximum_fusion.1), channel_id=1, source_target_pairs={{0,8},{1,17},{2,10},{3,19},{4,12},{5,21},{6,14},{7,23},{8,0},{9,25... | collective-permute-start | bytes 786440 | tf_op jit(solution)/shard_map/ppermute | solution.py:193
  22.5 7.4 %collective-permute-start.6 = (bf16[256,256]{1,0:T(8,128)(2,1)S(1)}, bf16[256,256]{1,0:T(8,128)(2,1)S(1)}, u32[]{:S(2)}, u32[]{:S(2)}) collective-permute-start(bf16[256,256]{1,0:T(8,128)(2,1)S(1)} %copy-done), channel_id=1, source_target_pairs={{0,8},{1,17},{2,10},{3,19},{4,12},{5,21},{6,14},{7,23},{8,0},{9,25... | collective-permute-start | bytes 393224 | tf_op jit(solution)/shard_map/ppermute | solution.py:193
  26.9 5.0 %collective-permute-start.14 = (bf16[256,256]{1,0:T(8,128)(2,1)S(1)}, bf16[256,256]{1,0:T(8,128)(2,1)S(1)}, u32[]{:S(2)}, u32[]{:S(2)}) collective-permute-start(bf16[256,256]{1,0:T(8,128)(2,1)S(1)} %collective-permute-done.13.refs_10_), channel_id=1, source_target_pairs={{0,8},{1,17},{2,10},{3,19},{4,12},{5,21},{6,14},{7,23},{8,0},{9,25... | collective-permute-start | bytes 393224 | tf_op jit(solution)/shard_map/ppermute | solution.py:193
  33.8 5.0 %collective-permute-start.17 = (bf16[256,256]{1,0:T(8,128)(2,1)S(1)}, bf16[256,256]{1,0:T(8,128)(2,1)S(1)}, u32[]{:S(2)}, u32[]{:S(2)}) collective-permute-start(bf16[256,256]{1,0:T(8,128)(2,1)S(1)} %fusion.11.refs_0_), channel_id=1, source_target_pairs={{0,16},{1,9},{2,18},{3,11},{4,20},{5,13},{6,22},{7,15},{8,24},{9,1... | collective-permute-start | bytes 393224 | tf_op jit(solution)/shard_map/ppermute | solution.py:193
  33.8 8.5 %collective-permute-start.18 = (bf16[256,256]{1,0:T(8,128)(2,1)S(1)}, bf16[256,256]{1,0:T(8,128)(2,1)S(1)}, u32[]{:S(2)}, u32[]{:S(2)}) collective-permute-start(bf16[256,256]{1,0:T(8,128)(2,1)S(1)} %fusion.11.refs_0_), channel_id=1, source_target_pairs={{0,2},{1,3},{2,0},{3,1},{4,6},{5,7},{6,4},{7,5},{8,10},{9,11},{10,... | collective-permute-start | bytes 393224 | tf_op jit(solution)/shard_map/ppermute | solution.py:193
  35.3 8.9 %collective-permute-start.20 = (bf16[256,256]{1,0:T(8,128)(2,1)S(1)}, bf16[256,256]{1,0:T(8,128)(2,1)S(1)}, u32[]{:S(2)}, u32[]{:S(2)}) collective-permute-start(bf16[256,256]{1,0:T(8,128)(2,1)S(1)} %fusion.11.refs_0_), channel_id=1, source_target_pairs={{0,4},{1,5},{2,6},{3,7},{4,0},{5,1},{6,2},{7,3},{8,12},{9,13},{10,... | collective-permute-start | bytes 393224 | tf_op jit(solution)/shard_map/ppermute | solution.py:193
  38.8 7.7 %collective-permute-start.22 = (bf16[256,256]{1,0:T(8,128)(2,1)S(1)}, bf16[256,256]{1,0:T(8,128)(2,1)S(1)}, u32[]{:S(2)}, u32[]{:S(2)}) collective-permute-start(bf16[256,256]{1,0:T(8,128)(2,1)S(1)} %collective-permute-done.17), channel_id=1, source_target_pairs={{0,2},{1,3},{2,0},{3,1},{4,6},{5,7},{6,4},{7,5},{8,10},{9,11},{10,... | collective-permute-start | bytes 393224 | tf_op jit(solution)/shard_map/ppermute | solution.py:193
  42.4 13.5 %collective-permute-start.19 = (bf16[512,256]{1,0:T(8,128)(2,1)S(1)}, bf16[512,256]{1,0:T(8,128)(2,1)S(1)}, u32[]{:S(2)}, u32[]{:S(2)}) collective-permute-start(bf16[512,256]{1,0:T(8,128)(2,1)S(1)} %constant_dynamic-update-slice_fusion.2.refs_2_), channel_id=1, source_target_pairs={{0,8},{1,17},{2,10},{3,19},{4,12},{5,21},{6,14},{7,23},{8,0},{9,25... | collective-permute-start | bytes 786440 | tf_op jit(solution)/shard_map/ppermute | solution.py:193
  44.1 6.4 %collective-permute-start.21 = (bf16[256,256]{1,0:T(8,128)(2,1)S(1)}, bf16[256,256]{1,0:T(8,128)(2,1)S(1)}, u32[]{:S(2)}, u32[]{:S(2)}) collective-permute-start(bf16[256,256]{1,0:T(8,128)(2,1)S(1)} %collective-permute-done.20.refs_0_), channel_id=1, source_target_pairs={{0,16},{1,9},{2,18},{3,11},{4,20},{5,13},{6,22},{7,15},{8,24},{9,1... | collective-permute-start | bytes 393224 | tf_op jit(solution)/shard_map/ppermute | solution.py:193
  44.3 6.4 %collective-permute-start.24 = (bf16[256,256]{1,0:T(8,128)(2,1)S(1)}, bf16[256,256]{1,0:T(8,128)(2,1)S(1)}, u32[]{:S(2)}, u32[]{:S(2)}) collective-permute-start(bf16[256,256]{1,0:T(8,128)(2,1)S(1)} %collective-permute-done.20.refs_0_), channel_id=1, source_target_pairs={{0,2},{1,3},{2,0},{3,1},{4,6},{5,7},{6,4},{7,5},{8,10},{9,11},{10,... | collective-permute-start | bytes 393224 | tf_op jit(solution)/shard_map/ppermute | solution.py:193
  46.5 10.1 %collective-permute-start.25 = (bf16[512,256]{1,0:T(8,128)(2,1)S(1)}, bf16[512,256]{1,0:T(8,128)(2,1)S(1)}, u32[]{:S(2)}, u32[]{:S(2)}) collective-permute-start(bf16[512,256]{1,0:T(8,128)(2,1)S(1)} %pad_maximum_fusion.2), channel_id=1, source_target_pairs={{0,8},{1,17},{2,10},{3,19},{4,12},{5,21},{6,14},{7,23},{8,0},{9,25... | collective-permute-start | bytes 786440 | tf_op jit(solution)/shard_map/ppermute | solution.py:193
  47.4 8.5 %collective-permute-start.16 = (bf16[256,256]{1,0:T(8,128)(2,1)S(1)}, bf16[256,256]{1,0:T(8,128)(2,1)S(1)}, u32[]{:S(2)}, u32[]{:S(2)}) collective-permute-start(bf16[256,256]{1,0:T(8,128)(2,1)S(1)} %fusion.11.refs_0_), channel_id=1, source_target_pairs={{0,8},{1,17},{2,10},{3,19},{4,12},{5,21},{6,14},{7,23},{8,0},{9,25... | collective-permute-start | bytes 393224 | tf_op jit(solution)/shard_map/ppermute | solution.py:193
  50.5 5.0 %collective-permute-start.23 = (bf16[256,256]{1,0:T(8,128)(2,1)S(1)}, bf16[256,256]{1,0:T(8,128)(2,1)S(1)}, u32[]{:S(2)}, u32[]{:S(2)}) collective-permute-start(bf16[256,256]{1,0:T(8,128)(2,1)S(1)} %collective-permute-done.21.refs_0_), channel_id=1, source_target_pairs={{0,2},{1,3},{2,0},{3,1},{4,6},{5,7},{6,4},{7,5},{8,10},{9,11},{10,... | collective-permute-start | bytes 393224 | tf_op jit(solution)/shard_map/ppermute | solution.py:193
  50.8 6.4 %collective-permute-start.26 = (bf16[512,256]{1,0:T(8,128)(2,1)S(1)}, bf16[512,256]{1,0:T(8,128)(2,1)S(1)}, u32[]{:S(2)}, u32[]{:S(2)}) collective-permute-start(bf16[512,256]{1,0:T(8,128)(2,1)S(1)} %pad_maximum_fusion.3), channel_id=1, source_target_pairs={{0,8},{1,17},{2,10},{3,19},{4,12},{5,21},{6,14},{7,23},{8,0},{9,25... | collective-permute-start | bytes 786440 | tf_op jit(solution)/shard_map/ppermute | solution.py:193
  (9 other events, 43.6 us)
